TPU v7x, 512 devices: a whole 4x8x8 slice. The times are simulated.
512 devices in a mesh: dp: 32 (over y, x), seq: 16 (over z, core).
Axes of the slice: x: 4, y: 8, z: 8, core: 2. Of those that a mesh axis runs over, the one named last changes fastest.
Arguments:
- tokens: bfloat16 [32, 4096, 2048], P('dp', 'seq'), may hold values from -6 to 6
- level_weights: float32 [32, 8, 21, 4096], P('dp', None, None, 'seq'), may hold values from 0.05 to 1
- w_query: bfloat16 [2048, 1024], P('dp'), may hold values from -0.125 to 0.125
- w_key: bfloat16 [2048, 1024], P('dp'), may hold values from -0.125 to 0.125
- w_value: bfloat16 [2048, 1024], P('dp'), may hold values from -0.125 to 0.125
- head_gain: float32 [1024], replicated, may hold values from 0.1 to 1.9
Outputs:
- attended: bfloat16 [32, 4096, 1024], P('dp', 'seq')
All inputs are finite; a program needn't handle non-finite values.
Results may differ from a plain program's by a relative error of at most 0.013.
Values may be sent and summed in bfloat16 or wider, within the bound.
No kernel may reach another device: no remote copies, remote signals or barrier semaphores. Data moves between devices by JAX's collectives and lax.ppermute only.
A program may use at most 64 MiB of HBM per device.

v0:
```python
import jax
import jax.numpy as jnp
from jax import lax
from jax.sharding import PartitionSpec as P

HEADS = 8
HEAD_DIM = 128


def level_onehot(length):
    position = jnp.arange(length, dtype=jnp.int32)
    xor_pos = jnp.bitwise_xor(position[:, None], position[None, :])
    level_depth = jnp.zeros((length, length), jnp.int32)
    bit_total = length.bit_length() - 1
    for level_bit in range(bit_total):
        level_depth = level_depth + (jnp.right_shift(xor_pos, level_bit) > 0).astype(jnp.int32)
    causal = position[None, :] <= position[:, None]
    tables = [
        jnp.where(causal & (level_depth == depth_value), 1.0, 0.0).astype(jnp.float32)
        for depth_value in range(bit_total + 1)
    ]
    return jnp.stack(tables)


def local(tokens, level_weights, w_query, w_key, w_value, head_gain):
    rows_here = tokens[0]
    weights_here = level_weights[0]
    tok_count = rows_here.shape[0]
    width = w_query.shape[1]
    low_bits = tok_count.bit_length() - 1
    stacked = jnp.stack([w_query, w_key, w_value])
    projected = jnp.einsum(
        "tn,knc->ktc",
        rows_here,
        lax.all_gather(stacked, "dp", axis=1, tiled=True),
        preferred_element_type=jnp.float32,
    )
    triple = projected.astype(jnp.bfloat16).reshape(3, tok_count, HEADS, HEAD_DIM)
    queries, keys_all, values_all = (triple[0], triple[1], triple[2])
    onehot = level_onehot(tok_count)
    scores = jnp.einsum("thd,shd->hts", queries, keys_all, preferred_element_type=jnp.float32)
    gating = jnp.einsum(
        "lts,hlt->hts", onehot, weights_here[:, : low_bits + 1, :], precision=lax.Precision.HIGHEST
    )
    mixing = (gating * scores).astype(jnp.bfloat16)
    summed = jnp.einsum("hts,shd->thd", mixing, values_all, preferred_element_type=jnp.float32)
    states = jnp.einsum("shd,she->hde", keys_all, values_all, preferred_element_type=jnp.float32)
    seq_bits = lax.axis_size("seq").bit_length() - 1
    seq_rank = lax.axis_index("seq")
    zeros_levels = jnp.zeros((seq_bits, HEADS, HEAD_DIM, HEAD_DIM), jnp.float32)
    shard_piece = lax.all_gather(
        states[None].astype(jnp.bfloat16), "seq", axis=0, tiled=True
    ).astype(jnp.float32)
    dev_ids = jnp.arange(shard_piece.shape[0], dtype=jnp.int32)
    member_rows = []
    for level_bit in range(seq_bits):
        same_top = jnp.right_shift(dev_ids, level_bit + 1) == jnp.right_shift(
            seq_rank, level_bit + 1
        )
        lower_half = jnp.bitwise_and(jnp.right_shift(dev_ids, level_bit), 1) == 0
        upper_half = jnp.bitwise_and(jnp.right_shift(seq_rank, level_bit), 1) == 1
        member_rows.append(
            jnp.where(same_top & lower_half & upper_half, 1.0, 0.0).astype(jnp.float32)
        )
    member = jnp.stack(member_rows)
    level_stack = zeros_levels + jnp.einsum(
        "bj,jhde->bhde", member, shard_piece, precision=lax.Precision.HIGHEST
    )
    level_half = level_stack.astype(jnp.bfloat16)
    remote = jnp.einsum("thd,lhde->lthe", queries, level_half, preferred_element_type=jnp.float32)
    level_scale = weights_here[:, low_bits + 1 : low_bits + 1 + seq_bits, :].transpose(1, 2, 0)[
        ..., None
    ]
    summed = summed + jnp.sum(remote * level_scale, axis=0)
    mean_square = jnp.mean(summed * summed, axis=-1, keepdims=True)
    normed = summed * lax.rsqrt(mean_square + 1e-06) * head_gain.reshape(HEADS, HEAD_DIM)
    return normed.reshape(1, tok_count, width).astype(jnp.bfloat16)


def solution(mesh):
    placed = (
        P("dp", "seq", None),
        P("dp", None, None, "seq"),
        P("dp", None),
        P("dp", None),
        P("dp", None),
        P(),
    )
    return jax.shard_map(
        local, mesh=mesh, in_specs=placed, out_specs=P("dp", "seq", None), check_vma=False
    )
```

profile of v0, /device:TPU:1, one launch (start us, length us, event | category | flops | bytes accessed | tf_op | source)
XLA Modules:
  0.0 221.3 jit_solution(12857224044191038440)
XLA Ops:
  6.5 0.0 copy-start
  6.5 0.0 all-gather.4.cloned.1.call-start
  6.5 1.9 pad_maximum_fusion
  8.4 0.0 all-gather.4.cloned.1.call-update
  8.5 0.0 all-gather.6.cloned.1.call-start
  8.5 131.9 %all-gather.4.cloned.1.call-done = bf16[3,2048,1024]{2,1,0:T(8,128)(2,1)} async-done(((bf16[3,64,1024]{2,1,0:T(8,128)(2,1)}), bf16[3,2048,1024]{2,1,0:T(8,128)(2,1)}) %all-gather.4.cloned.1.call-update) | async-done | bytes 12582928 | tf_op jit(solution)/shard_map/all_gather | solution.py:35
  140.4 0.0 copy-done
  140.4 8.3 %fusion.6 = bf16[3,256,1024]{1,2,0:T(8,128)(2,1)S(1)} fusion(bf16[3,2048,1024]{2,1,0:T(8,128)(2,1)} %all-gather.4.cloned.1.call-done, bf16[1,256,2048]{2,1,0:T(8,128)(2,1)S(1)} %copy-done), kind=kOutput, calls=%fused_computation.9 | convolution fusion | flops 3222011904 | bytes 15204352 | tf_op jit(solution)/shard_map/tn,knc->ktc/dot_general | solution.py:32
  148.7 0.0 copy-start.4
  148.7 0.9 fusion.26
  149.6 0.0 copy-start.1
  149.6 0.0 copy-start.2
  149.6 0.8 copy-done.1
  150.4 0.2 copy-done.2
  150.6 1.0 convolution_convert_fusion.1
  151.6 0.0 all-gather.6.cloned.1.call-update
  151.6 0.0 copy-done.4
  151.7 1.3 copy.16
  153.0 0.0 copy-start.3
  153.1 0.2 select_dynamic-update-slice_fusion.8
  153.3 0.2 select_dynamic-update-slice_fusion.7
  153.5 0.2 select_dynamic-update-slice_fusion.6
  153.8 0.2 select_dynamic-update-slice_fusion.5
  154.0 0.2 select_dynamic-update-slice_fusion.4
  154.3 0.2 select_dynamic-update-slice_fusion.3
  154.5 0.2 select_dynamic-update-slice_fusion.2
  154.7 0.2 select_dynamic-update-slice_fusion.1
  155.0 0.2 select_dynamic-update-slice_fusion
  155.2 0.0 copy-done.3
  155.2 4.9 %fusion.3 = f32[256,256,8]{1,2,0:T(8,128)S(1)} fusion(f32[8,9,256]{1,0,2:T(8,128)S(1)} %copy-done.3, f32[9,256,256]{2,1,0:T(8,128)S(1)} %select_dynamic-update-slice_fusion), kind=kOutput, calls=%fused_computation.4 | convolution fusion | flops 56623104 | bytes 4530176 | tf_op jit(solution)/shard_map/lts,hlt->hts/dot_general | solution.py:42
  160.2 35.6 %all-gather.6.cloned.1.call-done = bf16[128,128,128]{2,1,0:T(8,128)(2,1)} async-done(((bf16[8,128,128]{2,1,0:T(8,128)(2,1)}), bf16[128,128,128]{2,1,0:T(8,128)(2,1)}) %all-gather.6.cloned.1.call-update) | async-done | bytes 4194320 | tf_op jit(solution)/shard_map/all_gather | solution.py:51
  195.8 6.9 %fusion.1 = bf16[4,8,128,128]{3,0,2,1:T(4,128)(2,1)} fusion(bf16[16,8,128,128]{3,2,1,0:T(8,128)(2,1)} %bitcast.56, f32[1,16]{1,0:T(1,128)S(1)} %get-tuple-element.10, f32[1,16]{1,0:T(1,128)S(1)} %get-tuple-element.11, f32[1,16]{1,0:T(1,128)S(1)} %get-tuple-element.12, f32[1,16]{1,0:T(1,128)S(1)} %get-tuple-element.13), kind=kOutput, calls=%fused_computation.2 | convolution fusion | flops 100663488 | bytes 5243136 | tf_op jit(solution)/shard_map/bj,jhde->bhde/dot_general | solution.py:66
  202.7 2.3 %copy.21 = bf16[4,8,128,128]{2,3,0,1:T(8,128)(2,1)} copy(bf16[4,8,128,128]{3,0,2,1:T(4,128)(2,1)} %fusion.1) | data formatting | bytes 2097152 | tf_op jit(solution)/shard_map/bj,jhde->bhde/dot_general | solution.py:66
  205.0 3.1 %fusion = f32[256,8,128]{0,2,1:T(8,128)} fusion(bf16[256,8,128,1]{0,2,3,1:T(8,128)(2,1)} %bitcast.58, f32[4,256,8]{1,0,2:T(4,128)S(1)} %copy.13, bf16[4,8,128,128]{2,3,0,1:T(8,128)(2,1)} %copy.21), kind=kOutput, calls=%fused_computation.1 | convolution fusion | flops 270270464 | bytes 2654208 | tf_op jit(solution)/shard_map/thd,lhde->lthe/dot_general | solution.py:70
  208.1 0.0 copy-start.5
  208.1 3.9 %multiply_reduce_fusion = (f32[256,8]{0,1:T(8,128)S(1)}, f32[256,8,128]{0,2,1:T(8,128)}) fusion(f32[256,8,128]{0,2,1:T(8,128)} %fusion, bf16[256,8,128]{0,2,1:T(8,128)(2,1)} %bitcast.53, f32[256,256,8]{1,2,0:T(8,128)S(1)} %fusion.3, bf16[256,8,128]{0,2,1:T(8,128)(2,1)} %bitcast.59, bf16[256,8,128]{0,2,1:T(8,128)(2,1)} %bitcast.55), kind=kOutput, calls=%fused_computation.15 | convolution fusion | flops 270268416 | bytes 5775360 | tf_op jit(solution)/shard_map/hts,shd->thd/dot_general | solution.py:46
  212.0 0.0 copy-done.5
  212.0 1.4 multiply_convert_fusion
  213.4 1.0 copy.14
  (6 shorter events, 0.1 us)
Async XLA Ops:
  6.5 133.8 %copy-start = (bf16[1,256,2048]{2,1,0:T(8,128)(2,1)S(1)}, bf16[1,256,2048]{2,1,0:T(8,128)(2,1)}, u32[]{:S(2)}) copy-start(bf16[1,256,2048]{2,1,0:T(8,128)(2,1)} %param.6) | copy-start | bytes 3145732
  6.5 133.8 %all-gather.4.cloned.1.call-start = ((), (), s32[]{:S(2)}) async-start(), calls=%async_computation | async-start | bytes 12976128 | tf_op jit(solution)/shard_map/all_gather | solution.py:35
  8.5 187.3 %all-gather.6.cloned.1.call-start = ((), (), s32[]{:S(2)}) async-start(), calls=%async_computation.1 | async-start | bytes 4456448 | tf_op jit(solution)/shard_map/all_gather | solution.py:51
  148.7 2.9 %copy-start.4 = (f32[1,8,21,256]{3,1,2,0:T(8,128)S(1)}, f32[1,8,21,256]{3,1,2,0:T(8,128)}, u32[]{:S(2)}) copy-start(f32[1,8,21,256]{3,1,2,0:T(8,128)} %param.7) | copy-start | bytes 516100
  149.6 0.8 copy-start.1
  149.6 1.0 copy-start.2
  153.0 2.2 copy-start.3
  208.1 3.9 %copy-start.5 = (f32[1024]{0:T(1024)S(1)}, f32[1024]{0:T(1024)}, u32[]{:S(2)}) copy-start(f32[1024]{0:T(1024)} %param.11) | copy-start | bytes 12292
Sparse Core Ops, SparseCore 0:
  10.5 129.7 all-gather.3
  151.7 43.9 all-gather.5
where the time goes:
time: 222 us; the launch traced here: 221 us
  waiting for transfers between devices  168 us (76%)
  matrix products  28.2 us (13%)
  between operations  13.6 us (6%)
  local copies, waits for them, and re-layouts  6.55 us (3%)
  other arithmetic  5.46 us (2%)
    all_gather x1, waiting for transfers between devices, local(): lax.all_gather(stacked, 'dp', axis=1, tiled=True)  132 us
    all_gather x1, waiting for transfers between devices, local(): lax.all_gather(states[None].astype(jnp.bfloat16), 'seq', axis=0, tiled=True)  35.6 us
    dot_general x1, matrix products, local(): jnp.einsum('tn,knc->ktc', rows_here, lax.all_gather(stacked, 'dp', axis=1...  8.3 us
    dot_general x1, matrix products, local(): jnp.einsum('bj,jhde->bhde', member, shard_piece, precision=lax.Precision....  6.91 us
    dot_general x1, matrix products, local(): jnp.einsum('lts,hlt->hts', onehot, weights_here[:, :low_bits + 1, :], pre...  4.92 us
  transfers between devices with their start and end apart: 2, of which 2 were waited for; matrix products, arithmetic and copies ran while one was open for 4% of the time, Pallas kernels for 0%

commit v1 on v0

v1 whole, which is shorter than its diff:
```python
import jax
import jax.numpy as jnp
from jax import lax
from jax.experimental import pallas as pl
from jax.experimental.pallas import tpu as pltpu
from jax.sharding import Mesh, PartitionSpec as P

HEADS = 8
HEAD_DIM = 128
TOK = 256
LOW_LEVELS = 9
LEVEL_ROWS = 13
PAD_ROWS = 16
GROUP = 4
OWN_HEADS = HEADS // GROUP
OWN_COLS = OWN_HEADS * HEAD_DIM
Y, X = 8, 4
SHARD = 64
F32 = jnp.float32
BF16 = jnp.bfloat16


def dot(a, b, ca, cb):
    return lax.dot_general(a, b, (((ca,), (cb,)), ((), ())), preferred_element_type=F32)


def assemble(x_here, block, whole):
    for here in range(X):

        @pl.when(x_here == here)
        def _():
            for y in range(Y):
                for i in range(X):
                    start = (y * X + (here + i) % X) * SHARD
                    whole[start : start + SHARD, :] = block(y, i)


def kv_kernel(
    place, t0, t1, t2, t3, w0, w1, w2, w3, keys_out, values_out, near_state, pair_state, total, whole
):
    parts = (w0, w1, w2, w3)
    assemble(place[2], lambda y, i: parts[i][y * SHARD : (y + 1) * SHARD, :], whole)
    sums = []
    for j, tokens in enumerate((t0, t1, t2, t3)):
        both = dot(tokens[0:TOK, :], whole[...], 1, 0)
        keys_all = both[:, :OWN_COLS].astype(BF16)
        keys_out[j] = keys_all
        values_all = both[:, OWN_COLS:].T.astype(BF16)
        values_out[j] = values_all
        row = []
        for h in range(OWN_HEADS):
            cols = slice(h * HEAD_DIM, (h + 1) * HEAD_DIM)
            state = dot(values_all[cols], keys_all[:, cols], 1, 0)
            near_state[j, h] = state.astype(BF16)
            row.append(state)
        sums.append(row)
    for h in range(OWN_HEADS):
        low = sums[0][h] + sums[1][h]
        high = sums[2][h] + sums[3][h]
        pair_state[0, h] = low.astype(BF16)
        pair_state[1, h] = high.astype(BF16)
        total[h] = (low + high).astype(BF16)


def gated_quarter(scores, weights, xor_pos, causal, top):
    gate = jnp.broadcast_to(weights[top : top + 1, :], scores.shape)
    for level in range(top - 1, -1, -1):
        gate = jnp.where(xor_pos < 2**level, weights[level : level + 1, :], gate)
    return jnp.where(causal, gate * scores, 0.0).astype(BF16)


def level_weights_of(tokens, head):
    start = pl.multiple_of(head * TOK, TOK)
    return tokens[TOK : TOK + PAD_ROWS, pl.ds(start, TOK)].astype(F32)


def near_kernel(
    place, t0, t1, t2, t3, w, keys_in, values_in, near_state, pair_state, queries_out, part, whole
):
    assemble(place[2], lambda y, i: w[y, i * SHARD : (i + 1) * SHARD, :], whole)
    role = place[0]
    half = TOK // 2
    key_pos = lax.broadcasted_iota(jnp.int32, (half, half), 0)
    query_pos = lax.broadcasted_iota(jnp.int32, (half, half), 1)
    xor_pos = jnp.bitwise_xor(key_pos, query_pos)
    causal = key_pos <= query_pos
    for j, tokens in enumerate((t0, t1, t2, t3)):
        block = jnp.bitwise_xor(role, j)
        use = (
            jnp.bitwise_and(block, 1).astype(F32),
            jnp.right_shift(block, 1).astype(F32),
        )
        queries_all = dot(tokens[0:TOK, :], whole[...], 1, 0).astype(BF16)
        queries_out[j] = queries_all
        for h in range(OWN_HEADS):
            cols = slice(h * HEAD_DIM, (h + 1) * HEAD_DIM)
            queries = queries_all[:, cols]
            keys = keys_in[j, :, cols]
            values = values_in[j, cols, :]
            weights = level_weights_of(tokens, role * OWN_HEADS + h)
            first = dot(keys[:half], queries, 1, 1)
            second = dot(keys[half:], queries[half:], 1, 1)
            mixed_00 = gated_quarter(first[:, :half], weights[:, :half], xor_pos, causal, 7)
            mixed_01 = (first[:, half:] * weights[8:9, half:]).astype(BF16)
            mixed_11 = gated_quarter(second, weights[:, half:], xor_pos, causal, 7)
            near_0 = dot(values[:, :half], mixed_00, 1, 0)
            near_1 = dot(values, jnp.concatenate([mixed_01, mixed_11], 0), 1, 0)
            summed = jnp.concatenate([near_0, near_1], 1)
            states = jnp.concatenate([near_state[j ^ 1, h], pair_state[(j >> 1) ^ 1, h]], 0)
            remote = dot(states, queries, 1, 1)
            for i in range(2):
                row = LOW_LEVELS + i
                summed = summed + remote[i * HEAD_DIM : (i + 1) * HEAD_DIM] * (
                    weights[row : row + 1, :] * use[i]
                )
            part[j, h] = summed


def finish_kernel(place, t0, t1, t2, t3, queries_in, part, far_1, far_2, far_3, gain, out):
    role = place[0]
    group = place[1]
    use = (jnp.bitwise_and(group, 1).astype(F32), jnp.right_shift(group, 1).astype(F32))
    for h in range(OWN_HEADS):
        head = role * OWN_HEADS + h
        cols = slice(h * HEAD_DIM, (h + 1) * HEAD_DIM)
        far_high = (far_2[h].astype(F32) + far_3[h].astype(F32)).astype(BF16)
        states = jnp.concatenate([far_1[h], far_high], 0)
        for j, tokens in enumerate((t0, t1, t2, t3)):
            block = jnp.bitwise_xor(role, j)
            weights = level_weights_of(tokens, head)
            remote = dot(states, queries_in[j, :, cols], 1, 1)
            summed = part[j, h]
            for i in range(2):
                row = LOW_LEVELS + 2 + i
                summed = summed + remote[i * HEAD_DIM : (i + 1) * HEAD_DIM] * (
                    weights[row : row + 1, :] * use[i]
                )
            mean_square = jnp.mean(summed * summed, axis=0, keepdims=True)
            normed = (summed * lax.rsqrt(mean_square + 1e-06)).T * gain[head]
            out[block, :, cols] = normed.astype(BF16)


VMEM = pl.BlockSpec(memory_space=pltpu.VMEM)
SMEM = pl.BlockSpec(memory_space=pltpu.SMEM)


def swap(array, axis, size, bit):
    return lax.ppermute(array, axis, [(i, i ^ bit) for i in range(size)])


def spread_over(array, axis, size):
    return lax.all_to_all(
        jnp.broadcast_to(array[None], (size,) + array.shape), axis, 0, 0, tiled=True
    )


def from_other_x(line):
    return [
        lax.ppermute(line, "x", [((i + shift) % X, i) for i in range(X)]) for shift in range(1, X)
    ]


def call(kernel, name, outs, ins, scratch=(), flops=0):
    return pl.pallas_call(
        kernel,
        out_shape=[jax.ShapeDtypeStruct(shape, dtype) for shape, dtype in outs],
        in_specs=[SMEM if array.dtype == jnp.int32 else VMEM for array in ins],
        out_specs=[VMEM] * len(outs),
        scratch_shapes=list(scratch),
        compiler_params=pltpu.CompilerParams(vmem_limit_bytes=16 * 2**20),
        cost_estimate=pl.CostEstimate(flops=flops, bytes_accessed=8 * 2**20, transcendentals=0),
        name=name,
    )(*ins)


def local(tokens, level_weights, w_query, w_key, w_value, head_gain):
    role = lax.axis_index(("zl", "c"))
    group = lax.axis_index("zh")
    place = jnp.stack([role, group, lax.axis_index("x")]).astype(jnp.int32)
    used = level_weights[0, :, :LEVEL_ROWS, :].astype(BF16)
    rows = used.transpose(1, 0, 2).reshape(LEVEL_ROWS, HEADS * TOK)
    packed = jnp.concatenate([tokens[0], jnp.pad(rows, ((0, PAD_ROWS - LEVEL_ROWS), (0, 0)))], 0)
    from_z = swap(packed, "zl", 2, 1)
    from_c = swap(packed, "c", 2, 1)

    def own(matrix):
        return lax.dynamic_slice_in_dim(matrix, role * OWN_COLS, OWN_COLS, 1)

    kv_line = spread_over(jnp.concatenate([own(w_key), own(w_value)], 1), "y", Y)
    kv_line = kv_line.reshape(Y * SHARD, 2 * OWN_COLS)
    q_here = own(w_query)
    q_row = jnp.concatenate([q_here] + from_other_x(q_here), 0)
    q_row, _ = lax.optimization_barrier((q_row, kv_line))
    q_all = spread_over(q_row, "y", Y)
    kv_other = from_other_x(kv_line)
    kv_kept, _ = lax.optimization_barrier((kv_line, q_all))
    kv_parts = [kv_kept] + kv_other
    from_zc = swap(from_z, "c", 2, 1)
    token_parts = (packed, from_c, from_z, from_zc)
    width = Y * X * SHARD
    state_shape = (OWN_HEADS, HEAD_DIM, HEAD_DIM)
    keys, values, near_state, pair_state, total = call(
        kv_kernel,
        "keys_values",
        [
            ((GROUP, TOK, OWN_COLS), BF16),
            ((GROUP, OWN_COLS, TOK), BF16),
            ((GROUP,) + state_shape, BF16),
            ((2,) + state_shape, BF16),
            (state_shape, BF16),
        ],
        [place, *token_parts, *kv_parts],
        [pltpu.VMEM((width, 2 * OWN_COLS), BF16)],
        2 * GROUP * TOK * width * 2 * OWN_COLS,
    )
    far = [swap(total, "zh", 4, bit) for bit in (1, 2, 3)]
    queries, part = call(
        near_kernel,
        "near",
        [((GROUP, TOK, OWN_COLS), BF16), ((GROUP, OWN_HEADS, HEAD_DIM, TOK), F32)],
        [place, *token_parts, q_all, keys, values, near_state, pair_state],
        [pltpu.VMEM((width, OWN_COLS), BF16)],
        2 * GROUP * TOK * width * OWN_COLS,
    )
    (out,) = call(
        finish_kernel,
        "finish",
        [((GROUP, TOK, OWN_COLS), BF16)],
        [place, *token_parts, queries, part, *far, head_gain.reshape(HEADS, 1, HEAD_DIM)],
        (),
        2 * GROUP * TOK * OWN_COLS * 2 * HEAD_DIM,
    )
    back = lax.all_to_all(out, ("zl", "c"), 0, 0, tiled=True)
    return back.transpose(1, 0, 2).reshape(1, TOK, HEADS * HEAD_DIM)


def solution(mesh):
    fine = Mesh(mesh.devices.reshape(Y, X, 4, 2, 2), ("y", "x", "zh", "zl", "c"))
    dp, seq = ("y", "x"), ("zh", "zl", "c")
    placed = (
        P(dp, seq, None),
        P(dp, None, None, seq),
        P(dp, None),
        P(dp, None),
        P(dp, None),
        P(),
    )
    return jax.shard_map(
        local, mesh=fine, in_specs=placed, out_specs=P(dp, seq, None), check_vma=False
    )
```

time: 222 us -> 118 us (0.53)
  waiting for transfers between devices: 168 us -> 21.2 us
  starting transfers between devices: 0.04 us -> 62.6 us
  matrix products: 28.2 us -> 0 us
  Pallas kernels: 0 us -> 13.6 us
  between operations: 13.6 us -> 0.26 us
  blocking collectives: 0 us -> 12.2 us
  other arithmetic: 5.46 us -> 0.21 us
    all_gather x2 -> x0, waiting for transfers between devices: 167 us -> none  [the longest x1 132 us: local(): lax.all_gather(stacked, 'dp', axis=1, tiled=True)]
    ppermute x0 -> x12, starting transfers between devices: none -> 48.4 us  [the longest x6 27.3 us: swap(): return lax.ppermute(array, axis, [(i, i ^ bit) for i in range(size)])]
    dot_general x6 -> x0, matrix products: 28.2 us -> none  [the longest x1 8.3 us: local(): jnp.einsum('tn,knc->ktc', rows_here, lax.all_gather(stacked, 'dp', axis=1...]
    all_to_all x0 -> x2, starting transfers between devices: none -> 14.3 us  [spread_over(): lax.all_to_all(jnp.broadcast_to(array[None], (size,) + array.shape), axis...]
    pallas_call x0 -> x3, Pallas kernels: none -> 13.6 us  [call(): pl.pallas_call(kernel, out_shape=[jax.ShapeDtypeStruct(shape, dtype) for...]
    all_to_all x0 -> x1, blocking collectives: none -> 12.2 us  [local(): back = lax.all_to_all(out, ('zl', 'c'), 0, 0, tiled=True)]
    ppermute x0 -> x12, waiting for transfers between devices: none -> 12.1 us  [the longest x6 12.1 us: from_other_x(): lax.ppermute(line, 'x', [((i + shift) % X, i) for i in range(X)])]
    all_to_all x0 -> x2, waiting for transfers between devices: none -> 9.12 us  [spread_over(): lax.all_to_all(jnp.broadcast_to(array[None], (size,) + array.shape), axis...]
  transfers between devices with their start and end apart: 2 -> 14, of which waited for: 2 -> 4; matrix products, arithmetic and copies ran while one was open for 4% -> 2% of each run, Pallas kernels for 0% -> 6%
where the time goes in v1:
time: 118 us; the launch traced here: 116 us
  starting transfers between devices  62.6 us (53%)
  waiting for transfers between devices  21.2 us (18%)
  Pallas kernels  13.6 us (12%)
  blocking collectives  12.2 us (10%)
  local copies, waits for them, and re-layouts  6.04 us (5%)
    ppermute x6, starting transfers between devices, swap(): return lax.ppermute(array, axis, [(i, i ^ bit) for i in range(size)])  27.3 us
    ppermute x6, starting transfers between devices, from_other_x(): lax.ppermute(line, 'x', [((i + shift) % X, i) for i in range(X)])  21.1 us
    all_to_all x2, starting transfers between devices, spread_over(): lax.all_to_all(jnp.broadcast_to(array[None], (size,) + array.shape), axis...  14.3 us
    pallas_call x3, Pallas kernels, call(): pl.pallas_call(kernel, out_shape=[jax.ShapeDtypeStruct(shape, dtype) for...  13.6 us
    all_to_all x1, blocking collectives, local(): back = lax.all_to_all(out, ('zl', 'c'), 0, 0, tiled=True)  12.2 us
    ppermute x6, waiting for transfers between devices, from_other_x(): lax.ppermute(line, 'x', [((i + shift) % X, i) for i in range(X)])  12.1 us
    all_to_all x2, waiting for transfers between devices, spread_over(): lax.all_to_all(jnp.broadcast_to(array[None], (size,) + array.shape), axis...  9.12 us
  transfers between devices with their start and end apart: 14, of which 4 were waited for; matrix products, arithmetic and copies ran while one was open for 2% of the time, Pallas kernels for 6%

profile of v1, /device:TPU:1, one launch (start us, length us, event | category | flops | bytes accessed | tf_op | source)
XLA Modules:
  0.0 116.2 jit_solution(15120050163808890819)
XLA Ops:
  0.0 0.0 copy-start
  0.0 0.9 constant_dynamic-slice_fusion
  0.9 0.8 broadcast_in_dim.4
  1.7 7.7 %all-to-all-start = ((bf16[8,64,512]{2,1,0:T(8,128)(2,1)}), bf16[8,64,512]{2,1,0:T(8,128)(2,1)S(1)}, u32[]{:S(2)}, u32[]{:S(2)}) async-start(bf16[8,64,512]{2,1,0:T(8,128)(2,1)} %broadcast_in_dim.4), calls=%async_computation | async-start | bytes 1048576 | tf_op jit(solution)/shard_map/all_to_all | solution.py:152
  9.4 0.9 fusion.2
  10.3 0.0 copy-done.4
  10.3 0.1 fusion.1.t0
  10.4 4.0 %collective-permute-start.1 = (bf16[272,2048]{1,0:T(8,128)(2,1)S(1)}, bf16[272,2048]{1,0:T(8,128)(2,1)S(1)}, u32[]{:S(2)}, u32[]{:S(2)}) collective-permute-start(bf16[272,2048]{1,0:T(8,128)(2,1)S(1)} %fusion.1.t0), channel_id=1, source_target_pairs={{0,2},{2,0},{1,3},{3,1},{4,6},{6,4},{5,7},{7,5},{8,10},{10,8},{9,1... | collective-permute-start | bytes 3342344 | tf_op jit(solution)/shard_map/ppermute | solution.py:148
  14.5 0.0 copy-done
  14.5 3.1 %collective-permute-start.5 = (bf16[64,256]{1,0:T(8,128)(2,1)S(1)}, bf16[64,256]{1,0:T(8,128)(2,1)S(1)}, u32[]{:S(2)}, u32[]{:S(2)}) collective-permute-start(bf16[64,256]{1,0:T(8,128)(2,1)S(1)} %constant_dynamic-slice_fusion.2), channel_id=1, source_target_pairs={{48,0},{0,16},{16,32},{32,48},{49,1},{1,17},{17,33},{33,49},{50,2}... | collective-permute-start | bytes 98312 | tf_op jit(solution)/shard_map/ppermute | solution.py:159
  17.6 4.4 %collective-permute-start.4 = (bf16[64,256]{1,0:T(8,128)(2,1)S(1)}, bf16[64,256]{1,0:T(8,128)(2,1)S(1)}, u32[]{:S(2)}, u32[]{:S(2)}) collective-permute-start(bf16[64,256]{1,0:T(8,128)(2,1)S(1)} %constant_dynamic-slice_fusion.2), channel_id=1, source_target_pairs={{32,0},{48,16},{0,32},{16,48},{33,1},{49,17},{1,33},{17,49},{34,2}... | collective-permute-start | bytes 98312 | tf_op jit(solution)/shard_map/ppermute | solution.py:159
  22.0 3.1 %collective-permute-start.3 = (bf16[64,256]{1,0:T(8,128)(2,1)S(1)}, bf16[64,256]{1,0:T(8,128)(2,1)S(1)}, u32[]{:S(2)}, u32[]{:S(2)}) collective-permute-start(bf16[64,256]{1,0:T(8,128)(2,1)S(1)} %constant_dynamic-slice_fusion.2), channel_id=1, source_target_pairs={{16,0},{32,16},{48,32},{0,48},{17,1},{33,17},{49,33},{1,49},{18,2}... | collective-permute-start | bytes 98312 | tf_op jit(solution)/shard_map/ppermute | solution.py:159
  25.0 0.0 collective-permute-done.5
  25.1 0.0 collective-permute-done.4
  25.1 1.9 %collective-permute-done.3 = bf16[64,256]{1,0:T(8,128)(2,1)S(1)} collective-permute-done((bf16[64,256]{1,0:T(8,128)(2,1)S(1)}, bf16[64,256]{1,0:T(8,128)(2,1)S(1)}, u32[]{:S(2)}, u32[]{:S(2)}) %collective-permute-start.3) | collective-permute-done | bytes 32800 | tf_op jit(solution)/shard_map/ppermute | solution.py:159
  26.9 0.0 all-to-all-done
  27.0 0.0 copy-start.1
  27.0 1.1 broadcast_in_dim.5
  28.1 0.0 copy-done.1
  28.1 6.6 %all-to-all-start.1 = ((bf16[8,256,256]{2,1,0:T(8,128)(2,1)}), bf16[8,256,256]{2,1,0:T(8,128)(2,1)}, u32[]{:S(2)}, u32[]{:S(2)}) async-start(bf16[8,256,256]{2,1,0:T(8,128)(2,1)} %broadcast_in_dim.5), calls=%async_computation.1 | async-start | bytes 2097152 | tf_op jit(solution)/shard_map/all_to_all | solution.py:152
  34.7 5.1 %collective-permute-start = (bf16[272,2048]{1,0:T(8,128)(2,1)S(1)}, bf16[272,2048]{1,0:T(8,128)(2,1)S(1)}, u32[]{:S(2)}, u32[]{:S(2)}) collective-permute-start(bf16[272,2048]{1,0:T(8,128)(2,1)S(1)} %fusion.1.t0), channel_id=1, source_target_pairs={{0,1},{1,0},{2,3},{3,2},{4,5},{5,4},{6,7},{7,6},{8,9},{9,8},{10,11... | collective-permute-start | bytes 3342344 | tf_op jit(solution)/shard_map/ppermute | solution.py:148
  39.9 0.0 collective-permute-done.1.t2
  39.9 2.0 %collective-permute-start.2 = (bf16[272,2048]{1,0:T(8,128)(2,1)S(1)}, bf16[272,2048]{1,0:T(8,128)(2,1)}, u32[]{:S(2)}, u32[]{:S(2)}) collective-permute-start(bf16[272,2048]{1,0:T(8,128)(2,1)S(1)} %collective-permute-done.1.t2), channel_id=1, source_target_pairs={{0,1},{1,0},{2,3},{3,2},{4,5},{5,4},{6,7},{7,6},{8,9},{9,8},{10,11... | collective-permute-start | bytes 3342344 | tf_op jit(solution)/shard_map/ppermute | solution.py:148
  41.9 3.1 %collective-permute-start.8 = (bf16[512,512]{1,0:T(8,128)(2,1)}, bf16[512,512]{1,0:T(8,128)(2,1)}, u32[]{:S(2)}, u32[]{:S(2)}) collective-permute-start(bf16[512,512]{1,0:T(8,128)(2,1)} %bitcast.15), channel_id=1, source_target_pairs={{48,0},{0,16},{16,32},{32,48},{49,1},{1,17},{17,33},{33,49},{50,2}... | collective-permute-start | bytes 1572872 | tf_op jit(solution)/shard_map/ppermute | solution.py:159
  45.0 4.4 %collective-permute-start.7 = (bf16[512,512]{1,0:T(8,128)(2,1)}, bf16[512,512]{1,0:T(8,128)(2,1)}, u32[]{:S(2)}, u32[]{:S(2)}) collective-permute-start(bf16[512,512]{1,0:T(8,128)(2,1)} %bitcast.16), channel_id=1, source_target_pairs={{32,0},{48,16},{0,32},{16,48},{33,1},{49,17},{1,33},{17,49},{34,2}... | collective-permute-start | bytes 1572872 | tf_op jit(solution)/shard_map/ppermute | solution.py:159
  49.4 3.1 %collective-permute-start.6 = (bf16[512,512]{1,0:T(8,128)(2,1)}, bf16[512,512]{1,0:T(8,128)(2,1)}, u32[]{:S(2)}, u32[]{:S(2)}) collective-permute-start(bf16[512,512]{1,0:T(8,128)(2,1)} %bitcast.17), channel_id=1, source_target_pairs={{16,0},{32,16},{48,32},{0,48},{17,1},{33,17},{49,33},{1,49},{18,2}... | collective-permute-start | bytes 1572872 | tf_op jit(solution)/shard_map/ppermute | solution.py:159
  52.4 0.1 pad_add_fusion.place
  52.5 9.1 %all-to-all-done.1.w = bf16[8,256,256]{2,1,0:T(8,128)(2,1)} async-done(((bf16[8,256,256]{2,1,0:T(8,128)(2,1)}), bf16[8,256,256]{2,1,0:T(8,128)(2,1)}, u32[]{:S(2)}, u32[]{:S(2)}) %all-to-all-start.1) | async-done | bytes 1048608 | tf_op jit(solution)/shard_map/all_to_all | solution.py:152
  61.6 0.0 collective-permute-done.t1
  61.6 0.0 collective-permute-done.8.w3
  61.6 9.1 %collective-permute-done.7.w2 = bf16[512,512]{1,0:T(8,128)(2,1)} collective-permute-done((bf16[512,512]{1,0:T(8,128)(2,1)}, bf16[512,512]{1,0:T(8,128)(2,1)}, u32[]{:S(2)}, u32[]{:S(2)}) %collective-permute-start.7) | collective-permute-done | bytes 524320 | tf_op jit(solution)/shard_map/ppermute | solution.py:159
  70.7 1.1 collective-permute-done.6.w1
  71.8 0.0 collective-permute-done.2.t3
  71.8 1.0 copy-done.2
  72.9 5.0 %keys_values.1 = (bf16[4,256,256]{2,1,0:T(8,128)(2,1)S(1)}, bf16[4,256,256]{2,1,0:T(8,128)(2,1)S(1)}, bf16[4,2,128,128]{3,2,1,0:T(8,128)(2,1)S(1)}, bf16[2,2,128...) custom-call(s32[3]{0:T(128)S(1)} %pad_add_fusion.place, bf16[272,2048]{1,0:T(8,128)(2,1)S(1)} %fusion.1.t0, ...), custom_call_target="tpu_custom_call" | custom-call | flops 2147483648 | bytes 8388608 | tf_op jit(solution)/shard_map/keys_values/pallas_call | solution.py:164
  77.9 10.3 %collective-permute-start.11 = (bf16[2,128,128]{2,1,0:T(8,128)(2,1)S(1)}, bf16[2,128,128]{2,1,0:T(8,128)(2,1)S(1)}, u32[]{:S(2)}, u32[]{:S(2)}) collective-permute-start(bf16[2,128,128]{2,1,0:T(8,128)(2,1)S(1)} %get-tuple-element.22), channel_id=1, source_target_pairs={{0,12},{4,8},{8,4},{12,0},{1,13},{5,9},{9,5},{13,1},{2,14},{6,10},... | collective-permute-start | bytes 196616 | tf_op jit(solution)/shard_map/ppermute | solution.py:148
  88.2 1.9 %collective-permute-start.10 = (bf16[2,128,128]{2,1,0:T(8,128)(2,1)S(1)}, bf16[2,128,128]{2,1,0:T(8,128)(2,1)S(1)}, u32[]{:S(2)}, u32[]{:S(2)}) collective-permute-start(bf16[2,128,128]{2,1,0:T(8,128)(2,1)S(1)} %get-tuple-element.22), channel_id=1, source_target_pairs={{0,8},{4,12},{8,0},{12,4},{1,9},{5,13},{9,1},{13,5},{2,10},{6,14},... | collective-permute-start | bytes 196616 | tf_op jit(solution)/shard_map/ppermute | solution.py:148
  90.1 4.0 %collective-permute-start.9 = (bf16[2,128,128]{2,1,0:T(8,128)(2,1)S(1)}, bf16[2,128,128]{2,1,0:T(8,128)(2,1)S(1)}, u32[]{:S(2)}, u32[]{:S(2)}) collective-permute-start(bf16[2,128,128]{2,1,0:T(8,128)(2,1)S(1)} %get-tuple-element.22), channel_id=1, source_target_pairs={{0,4},{4,0},{8,12},{12,8},{1,5},{5,1},{9,13},{13,9},{2,6},{6,2},{1... | collective-permute-start | bytes 196616 | tf_op jit(solution)/shard_map/ppermute | solution.py:148
  94.1 0.0 copy-start.3
  94.1 6.7 %near.1 = (bf16[4,256,256]{2,1,0:T(8,128)(2,1)S(1)}, f32[4,2,128,256]{3,2,1,0:T(8,128)S(1)}) custom-call(s32[3]{0:T(128)S(1)} %pad_add_fusion.place, bf16[272,2048]{1,0:T(8,128)(2,1)S(1)} %fusion.1.t0, bf16[272,2048]{1,0:T(8,128)(2,1)S(1)} %collective-permute-done.t1, bf16[272,2048]{1,0:T(8,128)(2,1)S(1)} %collective-permute-done.1.t2, ...), custom_call_target="tpu_custom_call" | custom-call | flops 1073741824 | bytes 8388608 | tf_op jit(solution)/shard_map/near/pallas_call | solution.py:164
  100.9 0.0 collective-permute-done.11.far_3
  100.9 0.0 collective-permute-done.10.far_2
  100.9 0.0 collective-permute-done.9.far_1
  100.9 0.0 copy-done.3
  100.9 1.9 %finish.1 = bf16[4,256,256]{2,1,0:T(8,128)(2,1)S(1)} custom-call(s32[3]{0:T(128)S(1)} %pad_add_fusion.place, bf16[272,2048]{1,0:T(8,128)(2,1)S(1)} %fusion.1.t0, bf16[272,2048]{1,0:T(8,128)(2,1)S(1)} %collective-permute-done.t1, bf16[272,2048]{1,0:T(8,128)(2,1)S(1)} %collective-permute-done.1.t2, bf16[272,2048]{1,0:T(8,128)(2,1)} %collective-permute-done.2.t3, ...), custom_call_target="tpu_custom_call" | custom-call | flops 134217728 | bytes 8388608 | tf_op jit(solution)/shard_map/finish/pallas_call | solution.py:164
  102.8 12.2 %all_to_all.15 = bf16[4,256,256]{2,1,0:T(8,128)(2,1)S(1)} all-to-all(bf16[4,256,256]{2,1,0:T(8,128)(2,1)S(1)} %finish.1), channel_id=1, replica_groups=mesh['y'=8,'x'=4,'zh'=4,'zl'=2,'c'=2] {'zl','c'}, dimensions={0} | all-to-all | bytes 1048576 | tf_op jit(solution)/shard_map/all_to_all | solution.py:233
  115.0 0.2 copy.7
  115.2 1.0 copy.8
  (7 shorter events, 0.1 us)
Async XLA Ops:
  0.0 14.5 %copy-start = (bf16[64,1024]{1,0:T(8,128)(2,1)S(1)}, bf16[64,1024]{1,0:T(8,128)(2,1)}, u32[]{:S(2)}) copy-start(bf16[64,1024]{1,0:T(8,128)(2,1)} %param.8) | copy-start | bytes 393220
  0.0 10.3 %copy-start.4 = (bf16[1,256,2048]{2,1,0:T(8,128)(2,1)S(1)}, bf16[1,256,2048]{2,1,0:T(8,128)(2,1)}, u32[]{:S(2)}) copy-start(bf16[1,256,2048]{2,1,0:T(8,128)(2,1)} %param.6) | copy-start | bytes 3145732
  1.7 25.2 %all-to-all-start = ((bf16[8,64,512]{2,1,0:T(8,128)(2,1)}), bf16[8,64,512]{2,1,0:T(8,128)(2,1)S(1)}, u32[]{:S(2)}, u32[]{:S(2)}) async-start(bf16[8,64,512]{2,1,0:T(8,128)(2,1)} %broadcast_in_dim.4), calls=%async_computation | async-start | bytes 1048576 | tf_op jit(solution)/shard_map/all_to_all | solution.py:152
  10.4 29.4 %collective-permute-start.1 = (bf16[272,2048]{1,0:T(8,128)(2,1)S(1)}, bf16[272,2048]{1,0:T(8,128)(2,1)S(1)}, u32[]{:S(2)}, u32[]{:S(2)}) collective-permute-start(bf16[272,2048]{1,0:T(8,128)(2,1)S(1)} %fusion.1.t0), channel_id=1, source_target_pairs={{0,2},{2,0},{1,3},{3,1},{4,6},{6,4},{5,7},{7,5},{8,10},{10,8},{9,1... | collective-permute-start | bytes 3342344 | tf_op jit(solution)/shard_map/ppermute | solution.py:148
  14.5 10.6 %collective-permute-start.5 = (bf16[64,256]{1,0:T(8,128)(2,1)S(1)}, bf16[64,256]{1,0:T(8,128)(2,1)S(1)}, u32[]{:S(2)}, u32[]{:S(2)}) collective-permute-start(bf16[64,256]{1,0:T(8,128)(2,1)S(1)} %constant_dynamic-slice_fusion.2), channel_id=1, source_target_pairs={{48,0},{0,16},{16,32},{32,48},{49,1},{1,17},{17,33},{33,49},{50,2}... | collective-permute-start | bytes 98312 | tf_op jit(solution)/shard_map/ppermute | solution.py:159
  17.6 7.4 %collective-permute-start.4 = (bf16[64,256]{1,0:T(8,128)(2,1)S(1)}, bf16[64,256]{1,0:T(8,128)(2,1)S(1)}, u32[]{:S(2)}, u32[]{:S(2)}) collective-permute-start(bf16[64,256]{1,0:T(8,128)(2,1)S(1)} %constant_dynamic-slice_fusion.2), channel_id=1, source_target_pairs={{32,0},{48,16},{0,32},{16,48},{33,1},{49,17},{1,33},{17,49},{34,2}... | collective-permute-start | bytes 98312 | tf_op jit(solution)/shard_map/ppermute | solution.py:159
  22.0 5.0 %collective-permute-start.3 = (bf16[64,256]{1,0:T(8,128)(2,1)S(1)}, bf16[64,256]{1,0:T(8,128)(2,1)S(1)}, u32[]{:S(2)}, u32[]{:S(2)}) collective-permute-start(bf16[64,256]{1,0:T(8,128)(2,1)S(1)} %constant_dynamic-slice_fusion.2), channel_id=1, source_target_pairs={{16,0},{32,16},{48,32},{0,48},{17,1},{33,17},{49,33},{1,49},{18,2}... | collective-permute-start | bytes 98312 | tf_op jit(solution)/shard_map/ppermute | solution.py:159
  27.0 1.1 copy-start.1
  28.1 33.5 %all-to-all-start.1 = ((bf16[8,256,256]{2,1,0:T(8,128)(2,1)}), bf16[8,256,256]{2,1,0:T(8,128)(2,1)}, u32[]{:S(2)}, u32[]{:S(2)}) async-start(bf16[8,256,256]{2,1,0:T(8,128)(2,1)} %broadcast_in_dim.5), calls=%async_computation.1 | async-start | bytes 2097152 | tf_op jit(solution)/shard_map/all_to_all | solution.py:152
  34.7 26.9 %collective-permute-start = (bf16[272,2048]{1,0:T(8,128)(2,1)S(1)}, bf16[272,2048]{1,0:T(8,128)(2,1)S(1)}, u32[]{:S(2)}, u32[]{:S(2)}) collective-permute-start(bf16[272,2048]{1,0:T(8,128)(2,1)S(1)} %fusion.1.t0), channel_id=1, source_target_pairs={{0,1},{1,0},{2,3},{3,2},{4,5},{5,4},{6,7},{7,6},{8,9},{9,8},{10,11... | collective-permute-start | bytes 3342344 | tf_op jit(solution)/shard_map/ppermute | solution.py:148
  39.9 32.0 %collective-permute-start.2 = (bf16[272,2048]{1,0:T(8,128)(2,1)S(1)}, bf16[272,2048]{1,0:T(8,128)(2,1)}, u32[]{:S(2)}, u32[]{:S(2)}) collective-permute-start(bf16[272,2048]{1,0:T(8,128)(2,1)S(1)} %collective-permute-done.1.t2), channel_id=1, source_target_pairs={{0,1},{1,0},{2,3},{3,2},{4,5},{5,4},{6,7},{7,6},{8,9},{9,8},{10,11... | collective-permute-start | bytes 3342344 | tf_op jit(solution)/shard_map/ppermute | solution.py:148
  41.9 19.8 %collective-permute-start.8 = (bf16[512,512]{1,0:T(8,128)(2,1)}, bf16[512,512]{1,0:T(8,128)(2,1)}, u32[]{:S(2)}, u32[]{:S(2)}) collective-permute-start(bf16[512,512]{1,0:T(8,128)(2,1)} %bitcast.15), channel_id=1, source_target_pairs={{48,0},{0,16},{16,32},{32,48},{49,1},{1,17},{17,33},{33,49},{50,2}... | collective-permute-start | bytes 1572872 | tf_op jit(solution)/shard_map/ppermute | solution.py:159
  45.0 25.7 %collective-permute-start.7 = (bf16[512,512]{1,0:T(8,128)(2,1)}, bf16[512,512]{1,0:T(8,128)(2,1)}, u32[]{:S(2)}, u32[]{:S(2)}) collective-permute-start(bf16[512,512]{1,0:T(8,128)(2,1)} %bitcast.16), channel_id=1, source_target_pairs={{32,0},{48,16},{0,32},{16,48},{33,1},{49,17},{1,33},{17,49},{34,2}... | collective-permute-start | bytes 1572872 | tf_op jit(solution)/shard_map/ppermute | solution.py:159
  49.4 22.5 %collective-permute-start.6 = (bf16[512,512]{1,0:T(8,128)(2,1)}, bf16[512,512]{1,0:T(8,128)(2,1)}, u32[]{:S(2)}, u32[]{:S(2)}) collective-permute-start(bf16[512,512]{1,0:T(8,128)(2,1)} %bitcast.17), channel_id=1, source_target_pairs={{16,0},{32,16},{48,32},{0,48},{17,1},{33,17},{49,33},{1,49},{18,2}... | collective-permute-start | bytes 1572872 | tf_op jit(solution)/shard_map/ppermute | solution.py:159
  71.8 1.0 copy-start.2
  77.9 23.0 %collective-permute-start.11 = (bf16[2,128,128]{2,1,0:T(8,128)(2,1)S(1)}, bf16[2,128,128]{2,1,0:T(8,128)(2,1)S(1)}, u32[]{:S(2)}, u32[]{:S(2)}) collective-permute-start(bf16[2,128,128]{2,1,0:T(8,128)(2,1)S(1)} %get-tuple-element.22), channel_id=1, source_target_pairs={{0,12},{4,8},{8,4},{12,0},{1,13},{5,9},{9,5},{13,1},{2,14},{6,10},... | collective-permute-start | bytes 196616 | tf_op jit(solution)/shard_map/ppermute | solution.py:148
  88.2 12.7 %collective-permute-start.10 = (bf16[2,128,128]{2,1,0:T(8,128)(2,1)S(1)}, bf16[2,128,128]{2,1,0:T(8,128)(2,1)S(1)}, u32[]{:S(2)}, u32[]{:S(2)}) collective-permute-start(bf16[2,128,128]{2,1,0:T(8,128)(2,1)S(1)} %get-tuple-element.22), channel_id=1, source_target_pairs={{0,8},{4,12},{8,0},{12,4},{1,9},{5,13},{9,1},{13,5},{2,10},{6,14},... | collective-permute-start | bytes 196616 | tf_op jit(solution)/shard_map/ppermute | solution.py:148
  90.1 10.8 %collective-permute-start.9 = (bf16[2,128,128]{2,1,0:T(8,128)(2,1)S(1)}, bf16[2,128,128]{2,1,0:T(8,128)(2,1)S(1)}, u32[]{:S(2)}, u32[]{:S(2)}) collective-permute-start(bf16[2,128,128]{2,1,0:T(8,128)(2,1)S(1)} %get-tuple-element.22), channel_id=1, source_target_pairs={{0,4},{4,0},{8,12},{12,8},{1,5},{5,1},{9,13},{13,9},{2,6},{6,2},{1... | collective-permute-start | bytes 196616 | tf_op jit(solution)/shard_map/ppermute | solution.py:148
  94.1 6.8 %copy-start.3 = (f32[1024]{0:T(1024)S(1)}, f32[1024]{0:T(1024)}, u32[]{:S(2)}) copy-start(f32[1024]{0:T(1024)} %param.11) | copy-start | bytes 12292

commit v2 on v1

v2 whole, which is shorter than its diff:
```python
import jax
import jax.numpy as jnp
from jax import lax
from jax.experimental import pallas as pl
from jax.experimental.pallas import tpu as pltpu
from jax.sharding import Mesh, PartitionSpec as P

HEADS = 8
HEAD_DIM = 128
TOK = 256
LOW_LEVELS = 9
LEVEL_ROWS = 13
PAD_ROWS = 16
GROUP = 4
OWN_HEADS = HEADS // GROUP
OWN_COLS = OWN_HEADS * HEAD_DIM
Y, X = 8, 4
SHARD = 64
FIRST = 4
CLASS_ROWS = Y * X * SHARD // 4
F32 = jnp.float32
BF16 = jnp.bfloat16


def dot(a, b, ca, cb):
    return lax.dot_general(a, b, (((ca,), (cb,)), ((), ())), preferred_element_type=F32)


def pack_kernel(place, tokens, level_weights, packed):
    for a in range(2):
        for b in range(2):
            apart = 2 * jnp.bitwise_xor(place[2], a) + jnp.bitwise_xor(place[3], b)
            for yh in range(Y // 2):
                pieces = []
                for xh in range(X // 2):
                    start = ((2 * yh + a) * X + 2 * xh) * SHARD
                    pair = tokens[:, start : start + 2 * SHARD]
                    pieces.append(pair[:, b * SHARD : (b + 1) * SHARD])
                to = pl.multiple_of(apart * CLASS_ROWS + yh * (X // 2) * SHARD, 2 * SHARD)
                packed[:TOK, pl.ds(to, 2 * SHARD)] = jnp.concatenate(pieces, 1)
    for h in range(HEADS):
        packed[TOK:, h * TOK : (h + 1) * TOK] = level_weights[:PAD_ROWS, h, :].astype(BF16)


def project_kernel(token_parts, weights, queries_out, keys_out, values_out, state_out):
    rows = jnp.concatenate([w[...] for w in weights], 0)
    states = []
    for j, tokens in enumerate(token_parts):
        every = dot(tokens[0:TOK, :], rows, 1, 0)
        both, queries = every[:, : 2 * OWN_COLS], every[:, 2 * OWN_COLS :]
        queries_out[j] = queries.astype(BF16)
        keys_all = both[:, :OWN_COLS].astype(BF16)
        keys_out[j] = keys_all
        values_all = both[:, OWN_COLS:].T.astype(BF16)
        values_out[j] = values_all
        row = []
        for h in range(OWN_HEADS):
            cols = slice(h * HEAD_DIM, (h + 1) * HEAD_DIM)
            row.append(dot(values_all[cols], keys_all[:, cols], 1, 0))
            state_out[j, h] = row[h].astype(BF16)
        states.append(row)
    return [states[0][h] + states[1][h] for h in range(OWN_HEADS)]


def first_kernel(t0, t1, w0, w1, w2, w3, queries_out, keys_out, values_out, state_out, pair_out, sum_out):
    sums = project_kernel((t0, t1), (w0, w1, w2, w3), queries_out, keys_out, values_out, state_out)
    for h in range(OWN_HEADS):
        pair_out[h] = sums[h].astype(BF16)
        sum_out[h] = sums[h]


def second_kernel(
    t2, t3, w0, w1, w2, w3, sum_in, queries_out, keys_out, values_out, state_out, pair_out, total
):
    sums = project_kernel((t2, t3), (w0, w1, w2, w3), queries_out, keys_out, values_out, state_out)
    for h in range(OWN_HEADS):
        pair_out[h] = sums[h].astype(BF16)
        both = (sums[h] + sum_in[h]).astype(BF16)
        for g in range(4):
            total[g, h] = both


def gated_quarter(scores, weights, xor_pos, causal, top):
    gate = jnp.broadcast_to(weights[top : top + 1, :], scores.shape)
    for level in range(top - 1, -1, -1):
        gate = jnp.where(xor_pos < 2**level, weights[level : level + 1, :], gate)
    return jnp.where(causal, gate * scores, 0.0).astype(BF16)


def attend_kernel(
    place, t0, t1, t2, t3, q0, q1, k0, k1, v0, v1, s0, s1, p0, p1, totals, gain, out, mixed
):
    queries_in, keys_in, values_in, near_state = (q0, q1), (k0, k1), (v0, v1), (s0, s1)
    pair_state = (p0, p1)
    role = place[0]
    group = place[1]
    half = TOK // 2
    key_pos = lax.broadcasted_iota(jnp.int32, (half, half), 0)
    query_pos = lax.broadcasted_iota(jnp.int32, (half, half), 1)
    xor_pos = jnp.bitwise_xor(key_pos, query_pos)
    causal = key_pos <= query_pos
    all_tokens = (t0, t1, t2, t3)

    def weights_of(j, h):
        start = pl.multiple_of((role * OWN_HEADS + h) * TOK, TOK)
        return all_tokens[j][TOK : TOK + PAD_ROWS, pl.ds(start, TOK)].astype(F32)

    for j in range(GROUP):
        for h in range(OWN_HEADS):
            cols = slice(h * HEAD_DIM, (h + 1) * HEAD_DIM)
            queries = queries_in[j >> 1][j & 1, :, cols]
            keys = keys_in[j >> 1][j & 1, :, cols]
            weights = weights_of(j, h)
            first = dot(keys[:half], queries, 1, 1)
            second = dot(keys[half:], queries[half:], 1, 1)
            mixed[j, h, :half, :half] = gated_quarter(first[:, :half], weights[:, :half], xor_pos, causal, 7)
            mixed[j, h, :half, half:] = (first[:, half:] * weights[8:9, half:]).astype(BF16)
            mixed[j, h, half:, half:] = gated_quarter(second, weights[:, half:], xor_pos, causal, 7)

    far_use = (jnp.bitwise_and(group, 1).astype(F32), jnp.right_shift(group, 1).astype(F32))
    for h in range(OWN_HEADS):
        head = role * OWN_HEADS + h
        cols = slice(h * HEAD_DIM, (h + 1) * HEAD_DIM)
        far_low = totals[jnp.bitwise_xor(group, 1), h]
        far_high = (totals[0, h].astype(F32) + totals[1, h].astype(F32)).astype(BF16)
        for j in range(GROUP):
            block = jnp.bitwise_xor(role, j)
            use = (
                jnp.bitwise_and(block, 1).astype(F32),
                jnp.right_shift(block, 1).astype(F32),
            ) + far_use
            weights = weights_of(j, h)
            states = jnp.concatenate(
                [near_state[j >> 1][(j & 1) ^ 1, h], pair_state[(j >> 1) ^ 1][h], far_low, far_high], 0
            )
            remote = dot(states, queries_in[j >> 1][j & 1, :, cols], 1, 1)
            values = values_in[j >> 1][j & 1, cols, :]
            near_0 = dot(values[:, :half], mixed[j, h, :half, :half], 1, 0)
            near_1 = dot(values, mixed[j, h, :, half:], 1, 0)
            summed = jnp.concatenate([near_0, near_1], 1)
            for i in range(4):
                row = LOW_LEVELS + i
                summed = summed + remote[i * HEAD_DIM : (i + 1) * HEAD_DIM] * (
                    weights[row : row + 1, :] * use[i]
                )
            mean_square = jnp.mean(summed * summed, axis=0, keepdims=True)
            normed = (summed * lax.rsqrt(mean_square + 1e-06)).T * gain[head]
            out[block, :, cols] = normed.astype(BF16)


VMEM = pl.BlockSpec(memory_space=pltpu.VMEM)
SMEM = pl.BlockSpec(memory_space=pltpu.SMEM)


def swap(array, axis, size, bit):
    return lax.ppermute(array, axis, [(i, i ^ bit) for i in range(size)])


def spread_over(array, axis, size):
    return lax.all_to_all(
        jnp.broadcast_to(array[None], (size,) + array.shape), axis, 0, 0, tiled=True
    )


def call(kernel, name, outs, ins, scratch=(), flops=0):
    return pl.pallas_call(
        kernel,
        out_shape=[jax.ShapeDtypeStruct(shape, dtype) for shape, dtype in outs],
        in_specs=[SMEM if array.dtype == jnp.int32 else VMEM for array in ins],
        out_specs=[VMEM] * len(outs),
        scratch_shapes=list(scratch),
        compiler_params=pltpu.CompilerParams(vmem_limit_bytes=16 * 2**20),
        cost_estimate=pl.CostEstimate(flops=flops, bytes_accessed=8 * 2**20, transcendentals=0),
        name=name,
    )(*ins)


def local(tokens, level_weights, w_query, w_key, w_value, head_gain):
    role = lax.axis_index(("zl", "c"))
    group = lax.axis_index("zh")
    place = jnp.stack([role, group, lax.axis_index("yl"), lax.axis_index("xl")]).astype(jnp.int32)
    def own(matrix):
        return lax.dynamic_slice_in_dim(matrix, role * OWN_COLS, OWN_COLS, 1)

    columns = jnp.concatenate([own(w_key), own(w_value), own(w_query)], 1)
    columns, tokens_later = lax.optimization_barrier((columns, tokens))
    (packed,) = call(
        pack_kernel,
        "pack",
        [((TOK + PAD_ROWS, Y * X * SHARD), BF16)],
        [place, tokens_later[0], level_weights[0].transpose(1, 0, 2)],
    )
    from_z = swap(packed, "zl", 2, 1)
    from_c = swap(packed, "c", 2, 1)
    same = spread_over(columns, ("yh", "xh"), Y * X // 4).reshape(CLASS_ROWS, 3 * OWN_COLS)
    from_x = lax.ppermute(same, ("xh", "xl"), [(i, (i + 1) % X) for i in range(X)])
    from_y = lax.ppermute(same, ("yh", "yl"), [(i, (i + 1) % Y) for i in range(Y)])
    from_yx = lax.ppermute(
        same,
        ("yh", "yl", "xh", "xl"),
        [(y * X + x, (y - 1) % Y * X + (x - 1) % X) for y in range(Y) for x in range(X)],
    )
    from_zc = swap(from_z, "c", 2, 1)
    token_parts = (packed, from_c, from_z, from_zc)
    weights = (same, from_x, from_y, from_yx)
    state_shape = (OWN_HEADS, HEAD_DIM, HEAD_DIM)
    results = [
        ((2, TOK, OWN_COLS), BF16),
        ((2, TOK, OWN_COLS), BF16),
        ((2, OWN_COLS, TOK), BF16),
        ((2,) + state_shape, BF16),
        (state_shape, BF16),
    ]
    flops = 2 * 2 * TOK * Y * X * SHARD * 3 * OWN_COLS
    *here, sum_here = call(
        first_kernel,
        "project_here",
        results + [(state_shape, F32)],
        [packed, from_c, *weights],
        (),
        FIRST * flops,
    )
    *there, total = call(
        second_kernel,
        "project_there",
        results + [((4,) + state_shape, BF16)],
        [from_z, from_zc, *weights, sum_here],
        (),
        flops,
    )
    totals = lax.all_to_all(total, "zh", 0, 0, tiled=True)
    (out,) = call(
        attend_kernel,
        "attend",
        [((GROUP, TOK, OWN_COLS), BF16)],
        [
            place,
            *token_parts,
            *[array for pair in zip(here, there) for array in pair],
            totals,
            head_gain.reshape(HEADS, 1, HEAD_DIM),
        ],
        [pltpu.VMEM((GROUP, OWN_HEADS, TOK, TOK), BF16)],
    )
    back = lax.all_to_all(out, ("zl", "c"), 0, 0, tiled=True)
    return back.transpose(1, 0, 2).reshape(1, TOK, HEADS * HEAD_DIM)


def solution(mesh):
    fine = Mesh(mesh.devices.reshape(Y // 2, 2, X // 2, 2, 4, 2, 2), ("yh", "yl", "xh", "xl", "zh", "zl", "c"))
    dp, seq = ("yh", "yl", "xh", "xl"), ("zh", "zl", "c")
    placed = (
        P(dp, seq, None),
        P(dp, None, None, seq),
        P(dp, None),
        P(dp, None),
        P(dp, None),
        P(),
    )
    return jax.shard_map(
        local, mesh=fine, in_specs=placed, out_specs=P(dp, seq, None), check_vma=False
    )
```

time: 118 us -> 106 us (0.90)
  starting transfers between devices: 62.6 us -> 29 us
  blocking collectives: 12.2 us -> 33.9 us
  waiting for transfers between devices: 21.2 us -> 27.7 us
  Pallas kernels: 13.6 us -> 9.53 us
  local copies, waits for them, and re-layouts: 6.04 us -> 3.9 us
    all_to_all x0 -> x1, blocking collectives: none -> 18.8 us  [local(): totals = lax.all_to_all(total, 'zh', 0, 0, tiled=True)]
    ppermute x6 -> x3, starting transfers between devices: 27.3 us -> 10.5 us  [swap(): return lax.ppermute(array, axis, [(i, i ^ bit) for i in range(size)])]
    ppermute x6 -> x3, starting transfers between devices: 21.1 us -> 8.36 us  [the longest x1 3.39 us: local(): lax.ppermute(same, ('xh', 'xl'), [(i, (i + 1) % X) for i in range(X)])]
    all_to_all x2 -> x1, waiting for transfers between devices: 9.12 us -> 14.7 us  [spread_over(): lax.all_to_all(jnp.broadcast_to(array[None], (size,) + array.shape), axis...]
    all_to_all x2 -> x1, starting transfers between devices: 14.3 us -> 10.1 us  [spread_over(): lax.all_to_all(jnp.broadcast_to(array[None], (size,) + array.shape), axis...]
    pallas_call x3 -> x4, Pallas kernels: 13.6 us -> 9.53 us  [call(): pl.pallas_call(kernel, out_shape=[jax.ShapeDtypeStruct(shape, dtype) for...]
    all_to_all x1, blocking collectives: 12.2 us -> 15.1 us  [local(): back = lax.all_to_all(out, ('zl', 'c'), 0, 0, tiled=True)]
    ppermute x6 -> x3, waiting for transfers between devices: 12.1 us -> 13 us  [the longest x1 9.71 us: local(): lax.ppermute(same, ('yh', 'yl', 'xh', 'xl'), [(y * X + x, (y - 1) % Y * X...]
  transfers between devices with their start and end apart: 14 -> 7, of which waited for: 4 -> 4; matrix products, arithmetic and copies ran while one was open for 2% -> 0% of each run, Pallas kernels for 6% -> 4%
where the time goes in v2:
time: 106 us; the launch traced here: 104 us
  blocking collectives  33.9 us (32%)
  starting transfers between devices  29 us (27%)
  waiting for transfers between devices  27.7 us (26%)
  Pallas kernels  9.53 us (9%)
  local copies, waits for them, and re-layouts  3.9 us (4%)
    all_to_all x1, blocking collectives, local(): totals = lax.all_to_all(total, 'zh', 0, 0, tiled=True)  18.8 us
    all_to_all x1, blocking collectives, local(): back = lax.all_to_all(out, ('zl', 'c'), 0, 0, tiled=True)  15.1 us
    all_to_all x1, waiting for transfers between devices, spread_over(): lax.all_to_all(jnp.broadcast_to(array[None], (size,) + array.shape), axis...  14.7 us
    ppermute x3, starting transfers between devices, swap(): return lax.ppermute(array, axis, [(i, i ^ bit) for i in range(size)])  10.5 us
    all_to_all x1, starting transfers between devices, spread_over(): lax.all_to_all(jnp.broadcast_to(array[None], (size,) + array.shape), axis...  10.1 us
    ppermute x1, waiting for transfers between devices, local(): lax.ppermute(same, ('yh', 'yl', 'xh', 'xl'), [(y * X + x, (y - 1) % Y * X...  9.71 us
    pallas_call x4, Pallas kernels, call(): pl.pallas_call(kernel, out_shape=[jax.ShapeDtypeStruct(shape, dtype) for...  9.53 us
    ppermute x1, starting transfers between devices, local(): lax.ppermute(same, ('xh', 'xl'), [(i, (i + 1) % X) for i in range(X)])  3.39 us
  transfers between devices with their start and end apart: 7, of which 4 were waited for; matrix products, arithmetic and copies ran while one was open for 0% of the time, Pallas kernels for 4%

profile of v2, /device:TPU:1, one launch (start us, length us, event | category | flops | bytes accessed | tf_op | source)
XLA Modules:
  0.0 104.3 jit_solution(16847825594148094653)
XLA Ops:
  0.0 0.0 copy-start
  0.0 0.9 copy-done
  0.9 0.8 constant_dynamic-slice_fusion
  1.7 0.0 copy-start.1
  1.7 0.0 copy-start.2
  1.7 1.0 broadcast_in_dim.2
  2.7 10.1 %all-to-all-start = ((bf16[8,64,768]{2,1,0:T(8,128)(2,1)}), bf16[8,64,768]{2,1,0:T(8,128)(2,1)}, u32[]{:S(2)}, u32[]{:S(2)}) async-start(bf16[8,64,768]{2,1,0:T(8,128)(2,1)} %broadcast_in_dim.2), calls=%async_computation | async-start | bytes 1572864 | tf_op jit(solution)/shard_map/all_to_all | solution.py:160
  12.8 0.1 pad_add_fusion.place
  12.9 0.0 copy-done.1
  12.9 0.0 copy-done.2
  12.9 1.0 pack.1.t0
  13.9 4.0 %collective-permute-start.1 = (bf16[272,2048]{1,0:T(8,128)(2,1)S(1)}, bf16[272,2048]{1,0:T(8,128)(2,1)S(1)}, u32[]{:S(2)}, u32[]{:S(2)}) collective-permute-start(bf16[272,2048]{1,0:T(8,128)(2,1)S(1)} %pack.1.t0), channel_id=1, source_target_pairs={{0,2},{2,0},{1,3},{3,1},{4,6},{6,4},{5,7},{7,5},{8,10},{10,8},{9,1... | collective-permute-start | bytes 3342344 | tf_op jit(solution)/shard_map/ppermute | solution.py:156
  18.0 3.1 %collective-permute-start = (bf16[272,2048]{1,0:T(8,128)(2,1)S(1)}, bf16[272,2048]{1,0:T(8,128)(2,1)S(1)}, u32[]{:S(2)}, u32[]{:S(2)}) collective-permute-start(bf16[272,2048]{1,0:T(8,128)(2,1)S(1)} %pack.1.t0), channel_id=1, source_target_pairs={{0,1},{1,0},{2,3},{3,2},{4,5},{5,4},{6,7},{7,6},{8,9},{9,8},{10,11... | collective-permute-start | bytes 3342344 | tf_op jit(solution)/shard_map/ppermute | solution.py:156
  21.1 14.7 %all-to-all-done = bf16[8,64,768]{2,1,0:T(8,128)(2,1)} async-done(((bf16[8,64,768]{2,1,0:T(8,128)(2,1)}), bf16[8,64,768]{2,1,0:T(8,128)(2,1)}, u32[]{:S(2)}, u32[]{:S(2)}) %all-to-all-start) | async-done | bytes 786464 | tf_op jit(solution)/shard_map/all_to_all | solution.py:160
  35.8 1.9 %collective-permute-start.5 = (bf16[512,768]{1,0:T(8,128)(2,1)}, bf16[512,768]{1,0:T(8,128)(2,1)S(1)}, u32[]{:S(2)}, u32[]{:S(2)}) collective-permute-start(bf16[512,768]{1,0:T(8,128)(2,1)} %bitcast.7.w0), channel_id=1, source_target_pairs={{0,496},{16,448},{32,464},{48,480},{64,48},{80,0},{96,16},{112,32}... | collective-permute-start | bytes 2359304 | tf_op jit(solution)/shard_map/ppermute | solution.py:198
  37.7 3.1 %collective-permute-start.4 = (bf16[512,768]{1,0:T(8,128)(2,1)}, bf16[512,768]{1,0:T(8,128)(2,1)S(1)}, u32[]{:S(2)}, u32[]{:S(2)}) collective-permute-start(bf16[512,768]{1,0:T(8,128)(2,1)} %bitcast.7.w0), channel_id=1, source_target_pairs={{0,64},{64,128},{128,192},{192,256},{256,320},{320,384},{384,448},... | collective-permute-start | bytes 2359304 | tf_op jit(solution)/shard_map/ppermute | solution.py:197
  40.8 3.4 %collective-permute-start.3 = (bf16[512,768]{1,0:T(8,128)(2,1)}, bf16[512,768]{1,0:T(8,128)(2,1)S(1)}, u32[]{:S(2)}, u32[]{:S(2)}) collective-permute-start(bf16[512,768]{1,0:T(8,128)(2,1)} %bitcast.7.w0), channel_id=1, source_target_pairs={{0,16},{16,32},{32,48},{48,0},{1,17},{17,33},{33,49},{49,1},{2,18}... | collective-permute-start | bytes 2359304 | tf_op jit(solution)/shard_map/ppermute | solution.py:196
  44.2 0.0 collective-permute-done.1.t2
  44.2 3.4 %collective-permute-start.2 = (bf16[272,2048]{1,0:T(8,128)(2,1)S(1)}, bf16[272,2048]{1,0:T(8,128)(2,1)S(1)}, u32[]{:S(2)}, u32[]{:S(2)}) collective-permute-start(bf16[272,2048]{1,0:T(8,128)(2,1)S(1)} %collective-permute-done.1.t2), channel_id=1, source_target_pairs={{0,1},{1,0},{2,3},{3,2},{4,5},{5,4},{6,7},{7,6},{8,9},{9,8},{10,11... | collective-permute-start | bytes 3342344 | tf_op jit(solution)/shard_map/ppermute | solution.py:156
  47.6 0.0 collective-permute-done.t1
  47.6 9.7 %collective-permute-done.5.w3 = bf16[512,768]{1,0:T(8,128)(2,1)S(1)} collective-permute-done((bf16[512,768]{1,0:T(8,128)(2,1)}, bf16[512,768]{1,0:T(8,128)(2,1)S(1)}, u32[]{:S(2)}, u32[]{:S(2)}) %collective-permute-start.5) | collective-permute-done | bytes 786464 | tf_op jit(solution)/shard_map/ppermute | solution.py:198
  57.3 2.2 %collective-permute-done.4.w2 = bf16[512,768]{1,0:T(8,128)(2,1)S(1)} collective-permute-done((bf16[512,768]{1,0:T(8,128)(2,1)}, bf16[512,768]{1,0:T(8,128)(2,1)S(1)}, u32[]{:S(2)}, u32[]{:S(2)}) %collective-permute-start.4) | collective-permute-done | bytes 786464 | tf_op jit(solution)/shard_map/ppermute | solution.py:197
  59.5 1.1 %collective-permute-done.3.w1 = bf16[512,768]{1,0:T(8,128)(2,1)S(1)} collective-permute-done((bf16[512,768]{1,0:T(8,128)(2,1)}, bf16[512,768]{1,0:T(8,128)(2,1)S(1)}, u32[]{:S(2)}, u32[]{:S(2)}) %collective-permute-start.3) | collective-permute-done | bytes 786464 | tf_op jit(solution)/shard_map/ppermute | solution.py:196
  60.6 3.1 %project_here.1 = (bf16[2,256,256]{2,1,0:T(8,128)(2,1)S(1)}, bf16[2,256,256]{2,1,0:T(8,128)(2,1)S(1)}, bf16[2,256,256]{2,1,0:T(8,128)(2,1)S(1)}, bf16[2,2,128,12...) custom-call(bf16[272,2048]{1,0:T(8,128)(2,1)S(1)} %pack.1.t0, ...), custom_call_target="tpu_custom_call" | custom-call | flops 6442450944 | bytes 8388608 | tf_op jit(solution)/shard_map/project_here/pallas_call | solution.py:166
  63.8 0.0 collective-permute-done.2.t3
  63.8 0.0 copy-start.3
  63.8 3.2 %project_there.1 = (bf16[2,256,256]{2,1,0:T(8,128)(2,1)S(1)}, bf16[2,256,256]{2,1,0:T(8,128)(2,1)S(1)}, bf16[2,256,256]{2,1,0:T(8,128)(2,1)S(1)}, bf16[2,2,128,1...) custom-call(bf16[272,2048]{1,0:T(8,128)(2,1)S(1)} %collective-permute-done.1.t2, ...), custom_call_target="tpu_custom_call" | custom-call | flops 1610612736 | bytes 8388608 | tf_op jit(solution)/shard_map/project_there/pallas_call | solution.py:166
  66.9 18.8 %all_to_all.15.totals = bf16[4,2,128,128]{3,2,1,0:T(8,128)(2,1)S(1)} all-to-all(bf16[4,2,128,128]{3,2,1,0:T(8,128)(2,1)S(1)} %get-tuple-element.32), channel_id=1, replica_groups=mesh['yh'=4,'yl'=2,'xh'=2,'xl'=2,'zh'=4,'zl'=2,'c'=2] {'zh'}, dimensions={0} | all-to-all | bytes 524288 | tf_op jit(solution)/shard_map/all_to_all | solution.py:231
  85.8 0.0 copy-done.3
  85.8 2.2 %attend.1 = bf16[4,256,256]{2,1,0:T(8,128)(2,1)S(1)} custom-call(s32[4]{0:T(128)S(1)} %pad_add_fusion.place, bf16[272,2048]{1,0:T(8,128)(2,1)S(1)} %pack.1.t0, bf16[272,2048]{1,0:T(8,128)(2,1)S(1)} %collective-permute-done.t1, bf16[272,2048]{1,0:T(8,128)(2,1)S(1)} %collective-permute-done.1.t2, bf16[272,2048]{1,0:T(8,128)(2,1)S(1)} %collective-permute-done.2.t3, ...), custom_call_target="tpu_custom_call" | custom-call | bytes 8388608 | tf_op jit(solution)/shard_map/attend/pallas_call | solution.py:166
  88.0 15.1 %all_to_all.16 = bf16[4,256,256]{2,1,0:T(8,128)(2,1)S(1)} all-to-all(bf16[4,256,256]{2,1,0:T(8,128)(2,1)S(1)} %attend.1), channel_id=1, replica_groups=mesh['yh'=4,'yl'=2,'xh'=2,'xl'=2,'zh'=4,'zl'=2,'c'=2] {'zl','c'}, dimensions={0} | all-to-all | bytes 1048576 | tf_op jit(solution)/shard_map/all_to_all | solution.py:245
  103.0 0.2 copy.7
  103.3 1.0 copy.8
  (2 shorter events, 0.0 us)
Async XLA Ops:
  0.0 0.9 copy-start
  1.7 11.2 %copy-start.1 = (bf16[1,256,2048]{2,1,0:T(8,128)(2,1)S(1)}, bf16[1,256,2048]{2,1,0:T(8,128)(2,1)}, u32[]{:S(2)}) copy-start(bf16[1,256,2048]{2,1,0:T(8,128)(2,1)} %param.6) | copy-start | bytes 3145732
  1.7 11.2 %copy-start.2 = (f32[1,8,21,256]{3,1,2,0:T(8,128)S(1)}, f32[1,8,21,256]{3,1,2,0:T(8,128)}, u32[]{:S(2)}) copy-start(f32[1,8,21,256]{3,1,2,0:T(8,128)} %param.7) | copy-start | bytes 516100
  2.7 33.1 %all-to-all-start = ((bf16[8,64,768]{2,1,0:T(8,128)(2,1)}), bf16[8,64,768]{2,1,0:T(8,128)(2,1)}, u32[]{:S(2)}, u32[]{:S(2)}) async-start(bf16[8,64,768]{2,1,0:T(8,128)(2,1)} %broadcast_in_dim.2), calls=%async_computation | async-start | bytes 1572864 | tf_op jit(solution)/shard_map/all_to_all | solution.py:160
  13.9 30.3 %collective-permute-start.1 = (bf16[272,2048]{1,0:T(8,128)(2,1)S(1)}, bf16[272,2048]{1,0:T(8,128)(2,1)S(1)}, u32[]{:S(2)}, u32[]{:S(2)}) collective-permute-start(bf16[272,2048]{1,0:T(8,128)(2,1)S(1)} %pack.1.t0), channel_id=1, source_target_pairs={{0,2},{2,0},{1,3},{3,1},{4,6},{6,4},{5,7},{7,5},{8,10},{10,8},{9,1... | collective-permute-start | bytes 3342344 | tf_op jit(solution)/shard_map/ppermute | solution.py:156
  18.0 29.6 %collective-permute-start = (bf16[272,2048]{1,0:T(8,128)(2,1)S(1)}, bf16[272,2048]{1,0:T(8,128)(2,1)S(1)}, u32[]{:S(2)}, u32[]{:S(2)}) collective-permute-start(bf16[272,2048]{1,0:T(8,128)(2,1)S(1)} %pack.1.t0), channel_id=1, source_target_pairs={{0,1},{1,0},{2,3},{3,2},{4,5},{5,4},{6,7},{7,6},{8,9},{9,8},{10,11... | collective-permute-start | bytes 3342344 | tf_op jit(solution)/shard_map/ppermute | solution.py:156
  35.8 21.5 %collective-permute-start.5 = (bf16[512,768]{1,0:T(8,128)(2,1)}, bf16[512,768]{1,0:T(8,128)(2,1)S(1)}, u32[]{:S(2)}, u32[]{:S(2)}) collective-permute-start(bf16[512,768]{1,0:T(8,128)(2,1)} %bitcast.7.w0), channel_id=1, source_target_pairs={{0,496},{16,448},{32,464},{48,480},{64,48},{80,0},{96,16},{112,32}... | collective-permute-start | bytes 2359304 | tf_op jit(solution)/shard_map/ppermute | solution.py:198
  37.7 21.8 %collective-permute-start.4 = (bf16[512,768]{1,0:T(8,128)(2,1)}, bf16[512,768]{1,0:T(8,128)(2,1)S(1)}, u32[]{:S(2)}, u32[]{:S(2)}) collective-permute-start(bf16[512,768]{1,0:T(8,128)(2,1)} %bitcast.7.w0), channel_id=1, source_target_pairs={{0,64},{64,128},{128,192},{192,256},{256,320},{320,384},{384,448},... | collective-permute-start | bytes 2359304 | tf_op jit(solution)/shard_map/ppermute | solution.py:197
  40.8 19.8 %collective-permute-start.3 = (bf16[512,768]{1,0:T(8,128)(2,1)}, bf16[512,768]{1,0:T(8,128)(2,1)S(1)}, u32[]{:S(2)}, u32[]{:S(2)}) collective-permute-start(bf16[512,768]{1,0:T(8,128)(2,1)} %bitcast.7.w0), channel_id=1, source_target_pairs={{0,16},{16,32},{32,48},{48,0},{1,17},{17,33},{33,49},{49,1},{2,18}... | collective-permute-start | bytes 2359304 | tf_op jit(solution)/shard_map/ppermute | solution.py:196
  44.2 19.5 %collective-permute-start.2 = (bf16[272,2048]{1,0:T(8,128)(2,1)S(1)}, bf16[272,2048]{1,0:T(8,128)(2,1)S(1)}, u32[]{:S(2)}, u32[]{:S(2)}) collective-permute-start(bf16[272,2048]{1,0:T(8,128)(2,1)S(1)} %collective-permute-done.1.t2), channel_id=1, source_target_pairs={{0,1},{1,0},{2,3},{3,2},{4,5},{5,4},{6,7},{7,6},{8,9},{9,8},{10,11... | collective-permute-start | bytes 3342344 | tf_op jit(solution)/shard_map/ppermute | solution.py:156
  63.8 22.0 %copy-start.3 = (f32[1024]{0:T(1024)S(1)}, f32[1024]{0:T(1024)}, u32[]{:S(2)}) copy-start(f32[1024]{0:T(1024)} %param.11) | copy-start | bytes 12292

commit v3 on v2

--- a/solution.py
+++ b/solution.py
@@ -42,40 +42,51 @@
         packed[TOK:, h * TOK : (h + 1) * TOK] = level_weights[:PAD_ROWS, h, :].astype(BF16)
 
 
-def project_kernel(token_parts, weights, queries_out, keys_out, values_out, state_out):
-    rows = jnp.concatenate([w[...] for w in weights], 0)
+def own_class_kernel(t0, t1, t2, w0, part_out, w_out):
+    for j, tokens in enumerate((t0, t1, t2)):
+        part_out[j] = dot(tokens[0:TOK, :CLASS_ROWS], w0[...], 1, 0)
+    w_out[...] = w0[...]
+
+
+def project_block(j, every, queries_out, keys_out, values_out, state_out):
+    both, queries = every[:, : 2 * OWN_COLS], every[:, 2 * OWN_COLS :]
+    queries_out[j] = queries.astype(BF16)
+    keys_all = both[:, :OWN_COLS].astype(BF16)
+    keys_out[j] = keys_all
+    values_all = both[:, OWN_COLS:].T.astype(BF16)
+    values_out[j] = values_all
     states = []
-    for j, tokens in enumerate(token_parts):
-        every = dot(tokens[0:TOK, :], rows, 1, 0)
-        both, queries = every[:, : 2 * OWN_COLS], every[:, 2 * OWN_COLS :]
-        queries_out[j] = queries.astype(BF16)
-        keys_all = both[:, :OWN_COLS].astype(BF16)
-        keys_out[j] = keys_all
-        values_all = both[:, OWN_COLS:].T.astype(BF16)
-        values_out[j] = values_all
-        row = []
-        for h in range(OWN_HEADS):
-            cols = slice(h * HEAD_DIM, (h + 1) * HEAD_DIM)
-            row.append(dot(values_all[cols], keys_all[:, cols], 1, 0))
-            state_out[j, h] = row[h].astype(BF16)
-        states.append(row)
-    return [states[0][h] + states[1][h] for h in range(OWN_HEADS)]
-
-
-def first_kernel(t0, t1, w0, w1, w2, w3, queries_out, keys_out, values_out, state_out, pair_out, sum_out):
-    sums = project_kernel((t0, t1), (w0, w1, w2, w3), queries_out, keys_out, values_out, state_out)
-    for h in range(OWN_HEADS):
-        pair_out[h] = sums[h].astype(BF16)
-        sum_out[h] = sums[h]
+    for h in range(OWN_HEADS):
+        cols = slice(h * HEAD_DIM, (h + 1) * HEAD_DIM)
+        state = dot(values_all[cols], keys_all[:, cols], 1, 0)
+        state_out[j, h] = state.astype(BF16)
+        states.append(state)
+    return states
+
+
+def first_kernel(t0, t1, part, w1, w2, w3, queries_out, keys_out, values_out, state_out, pair_out, sum_out):
+    rows = jnp.concatenate([w1[...], w2[...], w3[...]], 0)
+    outs = (queries_out, keys_out, values_out, state_out)
+    low, high = [
+        project_block(j, part[j] + dot(tokens[0:TOK, CLASS_ROWS:], rows, 1, 0), *outs)
+        for j, tokens in enumerate((t0, t1))
+    ]
+    for h in range(OWN_HEADS):
+        pair_out[h] = (low[h] + high[h]).astype(BF16)
+        sum_out[h] = low[h] + high[h]
 
 
 def second_kernel(
-    t2, t3, w0, w1, w2, w3, sum_in, queries_out, keys_out, values_out, state_out, pair_out, total
+    t2, t3, part, w0, w1, w2, w3, sum_in, queries_out, keys_out, values_out, state_out, pair_out, total
 ):
-    sums = project_kernel((t2, t3), (w0, w1, w2, w3), queries_out, keys_out, values_out, state_out)
-    for h in range(OWN_HEADS):
-        pair_out[h] = sums[h].astype(BF16)
-        both = (sums[h] + sum_in[h]).astype(BF16)
+    rows = jnp.concatenate([w1[...], w2[...], w3[...]], 0)
+    outs = (queries_out, keys_out, values_out, state_out)
+    low = project_block(0, part[2] + dot(t2[0:TOK, CLASS_ROWS:], rows, 1, 0), *outs)
+    rows = jnp.concatenate([w0[...], rows], 0)
+    high = project_block(1, dot(t3[0:TOK, :], rows, 1, 0), *outs)
+    for h in range(OWN_HEADS):
+        pair_out[h] = (low[h] + high[h]).astype(BF16)
+        both = (low[h] + high[h] + sum_in[h]).astype(BF16)
         for g in range(4):
             total[g, h] = both
 
@@ -103,7 +114,7 @@
 
     def weights_of(j, h):
         start = pl.multiple_of((role * OWN_HEADS + h) * TOK, TOK)
-        return all_tokens[j][TOK : TOK + PAD_ROWS, pl.ds(start, TOK)].astype(F32)
+        return all_tokens[j][:, pl.ds(start, TOK)].astype(F32)
 
     for j in range(GROUP):
         for h in range(OWN_HEADS):
@@ -162,14 +173,18 @@
     )
 
 
-def call(kernel, name, outs, ins, scratch=(), flops=0):
+LEVELS_OF = pl.BlockSpec((PAD_ROWS, Y * X * SHARD), lambda i: (TOK // PAD_ROWS, 0))
+
+
+def call(kernel, name, outs, ins, scratch=(), flops=0, specs={}):
     return pl.pallas_call(
         kernel,
         out_shape=[jax.ShapeDtypeStruct(shape, dtype) for shape, dtype in outs],
-        in_specs=[SMEM if array.dtype == jnp.int32 else VMEM for array in ins],
+        in_specs=[specs.get(i, SMEM if array.dtype == jnp.int32 else VMEM) for i, array in enumerate(ins)],
         out_specs=[VMEM] * len(outs),
+        grid=(1,) if specs else (),
         scratch_shapes=list(scratch),
-        compiler_params=pltpu.CompilerParams(vmem_limit_bytes=16 * 2**20),
+        compiler_params=pltpu.CompilerParams(vmem_limit_bytes=10 * 2**20),
         cost_estimate=pl.CostEstimate(flops=flops, bytes_accessed=8 * 2**20, transcendentals=0),
         name=name,
     )(*ins)
@@ -202,7 +217,16 @@
     )
     from_zc = swap(from_z, "c", 2, 1)
     token_parts = (packed, from_c, from_z, from_zc)
-    weights = (same, from_x, from_y, from_yx)
+    columns = 3 * OWN_COLS
+    part, same_here = call(
+        own_class_kernel,
+        "own_class",
+        [((3, TOK, columns), F32), ((CLASS_ROWS, columns), BF16)],
+        [packed, from_c, from_z, same],
+        (),
+        2 * 3 * TOK * CLASS_ROWS * columns,
+    )
+    others = (from_x, from_y, from_yx)
     state_shape = (OWN_HEADS, HEAD_DIM, HEAD_DIM)
     results = [
         ((2, TOK, OWN_COLS), BF16),
@@ -216,7 +240,7 @@
         first_kernel,
         "project_here",
         results + [(state_shape, F32)],
-        [packed, from_c, *weights],
+        [packed, from_c, part, *others],
         (),
         FIRST * flops,
     )
@@ -224,7 +248,7 @@
         second_kernel,
         "project_there",
         results + [((4,) + state_shape, BF16)],
-        [from_z, from_zc, *weights, sum_here],
+        [from_z, from_zc, part, same_here, *others, sum_here],
         (),
         flops,
     )
@@ -241,6 +265,7 @@
             head_gain.reshape(HEADS, 1, HEAD_DIM),
         ],
         [pltpu.VMEM((GROUP, OWN_HEADS, TOK, TOK), BF16)],
+        specs={i: LEVELS_OF for i in range(1, 1 + GROUP)},
     )
     back = lax.all_to_all(out, ("zl", "c"), 0, 0, tiled=True)
     return back.transpose(1, 0, 2).reshape(1, TOK, HEADS * HEAD_DIM)

time: 106 us -> 103 us (0.972)
  waiting for transfers between devices: 27.7 us -> 25.8 us
    ppermute x1, waiting for transfers between devices: 9.71 us -> 7.76 us  [local(): lax.ppermute(same, ('yh', 'yl', 'xh', 'xl'), [(y * X + x, (y - 1) % Y * X...]
    pallas_call x4 -> x5, Pallas kernels: 9.53 us -> 8.74 us  [call(): pl.pallas_call(kernel, out_shape=[jax.ShapeDtypeStruct(shape, dtype) for...]
  transfers between devices with their start and end apart: 7 -> 7, of which waited for: 4 -> 4; matrix products, arithmetic and copies ran while one was open for 0% -> 0% of each run, Pallas kernels for 4% -> 5%
where the time goes in v3:
time: 103 us; the launch traced here: 102 us
  blocking collectives  33.9 us (33%)
  starting transfers between devices  29 us (28%)
  waiting for transfers between devices  25.8 us (25%)
  Pallas kernels  8.74 us (8%)
  local copies, waits for them, and re-layouts  3.89 us (4%)
    all_to_all x1, blocking collectives, local(): totals = lax.all_to_all(total, 'zh', 0, 0, tiled=True)  18.8 us
    all_to_all x1, blocking collectives, local(): back = lax.all_to_all(out, ('zl', 'c'), 0, 0, tiled=True)  15.1 us
    all_to_all x1, waiting for transfers between devices, spread_over(): lax.all_to_all(jnp.broadcast_to(array[None], (size,) + array.shape), axis...  14.7 us
    ppermute x3, starting transfers between devices, swap(): return lax.ppermute(array, axis, [(i, i ^ bit) for i in range(size)])  10.5 us
    all_to_all x1, starting transfers between devices, spread_over(): lax.all_to_all(jnp.broadcast_to(array[None], (size,) + array.shape), axis...  10.1 us
    pallas_call x5, Pallas kernels, call(): pl.pallas_call(kernel, out_shape=[jax.ShapeDtypeStruct(shape, dtype) for...  8.74 us
    ppermute x1, waiting for transfers between devices, local(): lax.ppermute(same, ('yh', 'yl', 'xh', 'xl'), [(y * X + x, (y - 1) % Y * X...  7.76 us
    ppermute x1, starting transfers between devices, local(): lax.ppermute(same, ('xh', 'xl'), [(i, (i + 1) % X) for i in range(X)])  3.39 us
  transfers between devices with their start and end apart: 7, of which 4 were waited for; matrix products, arithmetic and copies ran while one was open for 0% of the time, Pallas kernels for 5%

profile of v3, /device:TPU:1, one launch (start us, length us, event | category | flops | bytes accessed | tf_op | source)
XLA Modules:
  0.0 101.5 jit_solution(3685501590187361454)
XLA Ops:
  0.0 0.0 copy-start
  0.0 0.9 copy-done
  0.9 0.8 constant_dynamic-slice_fusion
  1.7 0.0 copy-start.1
  1.7 0.0 copy-start.2
  1.7 1.0 broadcast_in_dim.2
  2.7 10.1 %all-to-all-start = ((bf16[8,64,768]{2,1,0:T(8,128)(2,1)}), bf16[8,64,768]{2,1,0:T(8,128)(2,1)}, u32[]{:S(2)}, u32[]{:S(2)}) async-start(bf16[8,64,768]{2,1,0:T(8,128)(2,1)} %broadcast_in_dim.2), calls=%async_computation | async-start | bytes 1572864 | tf_op jit(solution)/shard_map/all_to_all | solution.py:171
  12.8 0.1 pad_add_fusion.place
  12.9 0.0 copy-done.1
  12.9 0.0 copy-done.2
  12.9 1.0 %pack.1.t0 = bf16[272,2048]{1,0:T(8,128)(2,1)S(1)} custom-call(s32[4]{0:T(128)S(1)} %pad_add_fusion.place, bf16[256,2048]{1,0:T(8,128)(2,1)S(1)} %bitcast.12, f32[21,8,256]{2,1,0:T(8,128)S(1)} %bitcast.13), custom_call_target="tpu_custom_call" | custom-call | bytes 8388608 | tf_op jit(solution)/shard_map/pack/pallas_call | solution.py:180
  13.9 4.0 %collective-permute-start.1 = (bf16[272,2048]{1,0:T(8,128)(2,1)S(1)}, bf16[272,2048]{1,0:T(8,128)(2,1)S(1)}, u32[]{:S(2)}, u32[]{:S(2)}) collective-permute-start(bf16[272,2048]{1,0:T(8,128)(2,1)S(1)} %pack.1.t0), channel_id=1, source_target_pairs={{0,2},{2,0},{1,3},{3,1},{4,6},{6,4},{5,7},{7,5},{8,10},{10,8},{9,1... | collective-permute-start | bytes 3342344 | tf_op jit(solution)/shard_map/ppermute | solution.py:167
  18.0 3.1 %collective-permute-start = (bf16[272,2048]{1,0:T(8,128)(2,1)S(1)}, bf16[272,2048]{1,0:T(8,128)(2,1)S(1)}, u32[]{:S(2)}, u32[]{:S(2)}) collective-permute-start(bf16[272,2048]{1,0:T(8,128)(2,1)S(1)} %pack.1.t0), channel_id=1, source_target_pairs={{0,1},{1,0},{2,3},{3,2},{4,5},{5,4},{6,7},{7,6},{8,9},{9,8},{10,11... | collective-permute-start | bytes 3342344 | tf_op jit(solution)/shard_map/ppermute | solution.py:167
  21.1 14.7 %all-to-all-done = bf16[8,64,768]{2,1,0:T(8,128)(2,1)} async-done(((bf16[8,64,768]{2,1,0:T(8,128)(2,1)}), bf16[8,64,768]{2,1,0:T(8,128)(2,1)}, u32[]{:S(2)}, u32[]{:S(2)}) %all-to-all-start) | async-done | bytes 786464 | tf_op jit(solution)/shard_map/all_to_all | solution.py:171
  35.8 1.9 %collective-permute-start.5 = (bf16[512,768]{1,0:T(8,128)(2,1)}, bf16[512,768]{1,0:T(8,128)(2,1)S(1)}, u32[]{:S(2)}, u32[]{:S(2)}) collective-permute-start(bf16[512,768]{1,0:T(8,128)(2,1)} %bitcast.7.w0), channel_id=1, source_target_pairs={{0,496},{16,448},{32,464},{48,480},{64,48},{80,0},{96,16},{112,32}... | collective-permute-start | bytes 2359304 | tf_op jit(solution)/shard_map/ppermute | solution.py:213
  37.7 3.1 %collective-permute-start.4 = (bf16[512,768]{1,0:T(8,128)(2,1)}, bf16[512,768]{1,0:T(8,128)(2,1)S(1)}, u32[]{:S(2)}, u32[]{:S(2)}) collective-permute-start(bf16[512,768]{1,0:T(8,128)(2,1)} %bitcast.7.w0), channel_id=1, source_target_pairs={{0,64},{64,128},{128,192},{192,256},{256,320},{320,384},{384,448},... | collective-permute-start | bytes 2359304 | tf_op jit(solution)/shard_map/ppermute | solution.py:212
  40.8 3.4 %collective-permute-start.3 = (bf16[512,768]{1,0:T(8,128)(2,1)}, bf16[512,768]{1,0:T(8,128)(2,1)S(1)}, u32[]{:S(2)}, u32[]{:S(2)}) collective-permute-start(bf16[512,768]{1,0:T(8,128)(2,1)} %bitcast.7.w0), channel_id=1, source_target_pairs={{0,16},{16,32},{32,48},{48,0},{1,17},{17,33},{33,49},{49,1},{2,18}... | collective-permute-start | bytes 2359304 | tf_op jit(solution)/shard_map/ppermute | solution.py:211
  44.2 0.0 collective-permute-done.1.t2
  44.2 3.4 %collective-permute-start.2 = (bf16[272,2048]{1,0:T(8,128)(2,1)S(1)}, bf16[272,2048]{1,0:T(8,128)(2,1)S(1)}, u32[]{:S(2)}, u32[]{:S(2)}) collective-permute-start(bf16[272,2048]{1,0:T(8,128)(2,1)S(1)} %collective-permute-done.1.t2), channel_id=1, source_target_pairs={{0,1},{1,0},{2,3},{3,2},{4,5},{5,4},{6,7},{7,6},{8,9},{9,8},{10,11... | collective-permute-start | bytes 3342344 | tf_op jit(solution)/shard_map/ppermute | solution.py:167
  47.6 0.0 collective-permute-done.t1
  47.6 1.9 %own_class.1 = (f32[3,256,768]{2,1,0:T(8,128)S(1)}, bf16[512,768]{1,0:T(8,128)(2,1)S(1)}) custom-call(bf16[272,2048]{1,0:T(8,128)(2,1)S(1)} %pack.1.t0, bf16[272,2048]{1,0:T(8,128)(2,1)S(1)} %collective-permute-done.t1, bf16[272,2048]{1,0:T(8,128)(2,1)S(1)} %collective-permute-done.1.t2, bf16[512,768]{1,0:T(8,128)(2,1)} %bitcast.7.w0), custom_call_target="tpu_custom_call" | custom-call | flops 603979776 | bytes 8388608 | tf_op jit(solution)/shard_map/own_class/pallas_call | solution.py:180
  49.5 7.8 %collective-permute-done.5.w3 = bf16[512,768]{1,0:T(8,128)(2,1)S(1)} collective-permute-done((bf16[512,768]{1,0:T(8,128)(2,1)}, bf16[512,768]{1,0:T(8,128)(2,1)S(1)}, u32[]{:S(2)}, u32[]{:S(2)}) %collective-permute-start.5) | collective-permute-done | bytes 786464 | tf_op jit(solution)/shard_map/ppermute | solution.py:213
  57.3 2.2 %collective-permute-done.4.w2 = bf16[512,768]{1,0:T(8,128)(2,1)S(1)} collective-permute-done((bf16[512,768]{1,0:T(8,128)(2,1)}, bf16[512,768]{1,0:T(8,128)(2,1)S(1)}, u32[]{:S(2)}, u32[]{:S(2)}) %collective-permute-start.4) | collective-permute-done | bytes 786464 | tf_op jit(solution)/shard_map/ppermute | solution.py:212
  59.5 1.1 %collective-permute-done.3.w1 = bf16[512,768]{1,0:T(8,128)(2,1)S(1)} collective-permute-done((bf16[512,768]{1,0:T(8,128)(2,1)}, bf16[512,768]{1,0:T(8,128)(2,1)S(1)}, u32[]{:S(2)}, u32[]{:S(2)}) %collective-permute-start.3) | collective-permute-done | bytes 786464 | tf_op jit(solution)/shard_map/ppermute | solution.py:211
  60.6 1.6 %project_here.1 = (bf16[2,256,256]{2,1,0:T(8,128)(2,1)S(1)}, bf16[2,256,256]{2,1,0:T(8,128)(2,1)S(1)}, bf16[2,256,256]{2,1,0:T(8,128)(2,1)S(1)}, bf16[2,2,128,12...) custom-call(bf16[272,2048]{1,0:T(8,128)(2,1)S(1)} %pack.1.t0, ...), custom_call_target="tpu_custom_call" | custom-call | flops 6442450944 | bytes 8388608 | tf_op jit(solution)/shard_map/project_here/pallas_call | solution.py:180
  62.2 0.0 collective-permute-done.2.t3
  62.2 0.0 copy-start.3
  62.2 2.0 %project_there.1 = (bf16[2,256,256]{2,1,0:T(8,128)(2,1)S(1)}, bf16[2,256,256]{2,1,0:T(8,128)(2,1)S(1)}, bf16[2,256,256]{2,1,0:T(8,128)(2,1)S(1)}, bf16[2,2,128,1...) custom-call(bf16[272,2048]{1,0:T(8,128)(2,1)S(1)} %collective-permute-done.1.t2, ...), custom_call_target="tpu_custom_call" | custom-call | flops 1610612736 | bytes 8388608 | tf_op jit(solution)/shard_map/project_there/pallas_call | solution.py:180
  64.2 18.8 %all_to_all.15.totals = bf16[4,2,128,128]{3,2,1,0:T(8,128)(2,1)S(1)} all-to-all(bf16[4,2,128,128]{3,2,1,0:T(8,128)(2,1)S(1)} %get-tuple-element.36), channel_id=1, replica_groups=mesh['yh'=4,'yl'=2,'xh'=2,'xl'=2,'zh'=4,'zl'=2,'c'=2] {'zh'}, dimensions={0} | all-to-all | bytes 524288 | tf_op jit(solution)/shard_map/all_to_all | solution.py:255
  83.0 0.0 copy-done.3
  83.0 2.2 %attend.1 = bf16[4,256,256]{2,1,0:T(8,128)(2,1)S(1)} custom-call(s32[4]{0:T(128)S(1)} %pad_add_fusion.place, bf16[272,2048]{1,0:T(8,128)(2,1)S(1)} %pack.1.t0, bf16[272,2048]{1,0:T(8,128)(2,1)S(1)} %collective-permute-done.t1, bf16[272,2048]{1,0:T(8,128)(2,1)S(1)} %collective-permute-done.1.t2, bf16[272,2048]{1,0:T(8,128)(2,1)S(1)} %collective-permute-done.2.t3, ...), custom_call_target="tpu_custom_call" | custom-call | bytes 8388608 | tf_op jit(solution)/shard_map/attend/pallas_call | solution.py:180
  85.2 15.1 %all_to_all.16 = bf16[4,256,256]{2,1,0:T(8,128)(2,1)S(1)} all-to-all(bf16[4,256,256]{2,1,0:T(8,128)(2,1)S(1)} %attend.1), channel_id=1, replica_groups=mesh['yh'=4,'yl'=2,'xh'=2,'xl'=2,'zh'=4,'zl'=2,'c'=2] {'zl','c'}, dimensions={0} | all-to-all | bytes 1048576 | tf_op jit(solution)/shard_map/all_to_all | solution.py:270
  100.3 0.2 copy.7
  100.5 1.0 copy.8
  (2 shorter events, 0.0 us)
Async XLA Ops:
  0.0 0.9 copy-start
  1.7 11.2 %copy-start.1 = (bf16[1,256,2048]{2,1,0:T(8,128)(2,1)S(1)}, bf16[1,256,2048]{2,1,0:T(8,128)(2,1)}, u32[]{:S(2)}) copy-start(bf16[1,256,2048]{2,1,0:T(8,128)(2,1)} %param.6) | copy-start | bytes 3145732
  1.7 11.2 %copy-start.2 = (f32[1,8,21,256]{3,1,2,0:T(8,128)S(1)}, f32[1,8,21,256]{3,1,2,0:T(8,128)}, u32[]{:S(2)}) copy-start(f32[1,8,21,256]{3,1,2,0:T(8,128)} %param.7) | copy-start | bytes 516100
  2.7 33.1 %all-to-all-start = ((bf16[8,64,768]{2,1,0:T(8,128)(2,1)}), bf16[8,64,768]{2,1,0:T(8,128)(2,1)}, u32[]{:S(2)}, u32[]{:S(2)}) async-start(bf16[8,64,768]{2,1,0:T(8,128)(2,1)} %broadcast_in_dim.2), calls=%async_computation | async-start | bytes 1572864 | tf_op jit(solution)/shard_map/all_to_all | solution.py:171
  13.9 30.3 %collective-permute-start.1 = (bf16[272,2048]{1,0:T(8,128)(2,1)S(1)}, bf16[272,2048]{1,0:T(8,128)(2,1)S(1)}, u32[]{:S(2)}, u32[]{:S(2)}) collective-permute-start(bf16[272,2048]{1,0:T(8,128)(2,1)S(1)} %pack.1.t0), channel_id=1, source_target_pairs={{0,2},{2,0},{1,3},{3,1},{4,6},{6,4},{5,7},{7,5},{8,10},{10,8},{9,1... | collective-permute-start | bytes 3342344 | tf_op jit(solution)/shard_map/ppermute | solution.py:167
  18.0 29.6 %collective-permute-start = (bf16[272,2048]{1,0:T(8,128)(2,1)S(1)}, bf16[272,2048]{1,0:T(8,128)(2,1)S(1)}, u32[]{:S(2)}, u32[]{:S(2)}) collective-permute-start(bf16[272,2048]{1,0:T(8,128)(2,1)S(1)} %pack.1.t0), channel_id=1, source_target_pairs={{0,1},{1,0},{2,3},{3,2},{4,5},{5,4},{6,7},{7,6},{8,9},{9,8},{10,11... | collective-permute-start | bytes 3342344 | tf_op jit(solution)/shard_map/ppermute | solution.py:167
  35.8 21.5 %collective-permute-start.5 = (bf16[512,768]{1,0:T(8,128)(2,1)}, bf16[512,768]{1,0:T(8,128)(2,1)S(1)}, u32[]{:S(2)}, u32[]{:S(2)}) collective-permute-start(bf16[512,768]{1,0:T(8,128)(2,1)} %bitcast.7.w0), channel_id=1, source_target_pairs={{0,496},{16,448},{32,464},{48,480},{64,48},{80,0},{96,16},{112,32}... | collective-permute-start | bytes 2359304 | tf_op jit(solution)/shard_map/ppermute | solution.py:213
  37.7 21.8 %collective-permute-start.4 = (bf16[512,768]{1,0:T(8,128)(2,1)}, bf16[512,768]{1,0:T(8,128)(2,1)S(1)}, u32[]{:S(2)}, u32[]{:S(2)}) collective-permute-start(bf16[512,768]{1,0:T(8,128)(2,1)} %bitcast.7.w0), channel_id=1, source_target_pairs={{0,64},{64,128},{128,192},{192,256},{256,320},{320,384},{384,448},... | collective-permute-start | bytes 2359304 | tf_op jit(solution)/shard_map/ppermute | solution.py:212
  40.8 19.8 %collective-permute-start.3 = (bf16[512,768]{1,0:T(8,128)(2,1)}, bf16[512,768]{1,0:T(8,128)(2,1)S(1)}, u32[]{:S(2)}, u32[]{:S(2)}) collective-permute-start(bf16[512,768]{1,0:T(8,128)(2,1)} %bitcast.7.w0), channel_id=1, source_target_pairs={{0,16},{16,32},{32,48},{48,0},{1,17},{17,33},{33,49},{49,1},{2,18}... | collective-permute-start | bytes 2359304 | tf_op jit(solution)/shard_map/ppermute | solution.py:211
  44.2 18.0 %collective-permute-start.2 = (bf16[272,2048]{1,0:T(8,128)(2,1)S(1)}, bf16[272,2048]{1,0:T(8,128)(2,1)S(1)}, u32[]{:S(2)}, u32[]{:S(2)}) collective-permute-start(bf16[272,2048]{1,0:T(8,128)(2,1)S(1)} %collective-permute-done.1.t2), channel_id=1, source_target_pairs={{0,1},{1,0},{2,3},{3,2},{4,5},{5,4},{6,7},{7,6},{8,9},{9,8},{10,11... | collective-permute-start | bytes 3342344 | tf_op jit(solution)/shard_map/ppermute | solution.py:167
  62.2 20.8 %copy-start.3 = (f32[1024]{0:T(1024)S(1)}, f32[1024]{0:T(1024)}, u32[]{:S(2)}) copy-start(f32[1024]{0:T(1024)} %param.11) | copy-start | bytes 12292

commit v4 on v3

--- a/solution.py
+++ b/solution.py
@@ -48,6 +48,12 @@
     w_out[...] = w0[...]
 
 
+def two_classes_kernel(t0, t1, t2, part, w2, w3, part_out):
+    rows = jnp.concatenate([w2[...], w3[...]], 0)
+    for j, tokens in enumerate((t0, t1, t2)):
+        part_out[j] = part[j] + dot(tokens[0:TOK, 2 * CLASS_ROWS :], rows, 1, 0)
+
+
 def project_block(j, every, queries_out, keys_out, values_out, state_out):
     both, queries = every[:, : 2 * OWN_COLS], every[:, 2 * OWN_COLS :]
     queries_out[j] = queries.astype(BF16)
@@ -64,11 +70,10 @@
     return states
 
 
-def first_kernel(t0, t1, part, w1, w2, w3, queries_out, keys_out, values_out, state_out, pair_out, sum_out):
-    rows = jnp.concatenate([w1[...], w2[...], w3[...]], 0)
+def first_kernel(t0, t1, part, w1, queries_out, keys_out, values_out, state_out, pair_out, sum_out):
     outs = (queries_out, keys_out, values_out, state_out)
     low, high = [
-        project_block(j, part[j] + dot(tokens[0:TOK, CLASS_ROWS:], rows, 1, 0), *outs)
+        project_block(j, part[j] + dot(tokens[0:TOK, CLASS_ROWS : 2 * CLASS_ROWS], w1[...], 1, 0), *outs)
         for j, tokens in enumerate((t0, t1))
     ]
     for h in range(OWN_HEADS):
@@ -79,10 +84,9 @@
 def second_kernel(
     t2, t3, part, w0, w1, w2, w3, sum_in, queries_out, keys_out, values_out, state_out, pair_out, total
 ):
-    rows = jnp.concatenate([w1[...], w2[...], w3[...]], 0)
     outs = (queries_out, keys_out, values_out, state_out)
-    low = project_block(0, part[2] + dot(t2[0:TOK, CLASS_ROWS:], rows, 1, 0), *outs)
-    rows = jnp.concatenate([w0[...], rows], 0)
+    low = project_block(0, part[2] + dot(t2[0:TOK, CLASS_ROWS : 2 * CLASS_ROWS], w1[...], 1, 0), *outs)
+    rows = jnp.concatenate([w0[...], w1[...], w2[...], w3[...]], 0)
     high = project_block(1, dot(t3[0:TOK, :], rows, 1, 0), *outs)
     for h in range(OWN_HEADS):
         pair_out[h] = (low[h] + high[h]).astype(BF16)
@@ -176,7 +180,7 @@
 LEVELS_OF = pl.BlockSpec((PAD_ROWS, Y * X * SHARD), lambda i: (TOK // PAD_ROWS, 0))
 
 
-def call(kernel, name, outs, ins, scratch=(), flops=0, specs={}):
+def call(kernel, name, outs, ins, scratch=(), flops=0, specs={}, traffic=8 * 2**20):
     return pl.pallas_call(
         kernel,
         out_shape=[jax.ShapeDtypeStruct(shape, dtype) for shape, dtype in outs],
@@ -185,9 +189,14 @@
         grid=(1,) if specs else (),
         scratch_shapes=list(scratch),
         compiler_params=pltpu.CompilerParams(vmem_limit_bytes=10 * 2**20),
-        cost_estimate=pl.CostEstimate(flops=flops, bytes_accessed=8 * 2**20, transcendentals=0),
+        cost_estimate=pl.CostEstimate(flops=flops, bytes_accessed=traffic, transcendentals=0),
         name=name,
     )(*ins)
+
+
+def join_kernel(back, out):
+    for r in range(GROUP):
+        out[:, r * OWN_COLS : (r + 1) * OWN_COLS] = back[r]
 
 
 def local(tokens, level_weights, w_query, w_key, w_value, head_gain):
@@ -227,6 +236,13 @@
         2 * 3 * TOK * CLASS_ROWS * columns,
     )
     others = (from_x, from_y, from_yx)
+    (part,) = call(
+        two_classes_kernel,
+        "two_classes",
+        [((3, TOK, columns), F32)],
+        [packed, from_c, from_z, part, from_y, from_yx],
+        traffic=0,
+    )
     state_shape = (OWN_HEADS, HEAD_DIM, HEAD_DIM)
     results = [
         ((2, TOK, OWN_COLS), BF16),
@@ -240,7 +256,7 @@
         first_kernel,
         "project_here",
         results + [(state_shape, F32)],
-        [packed, from_c, part, *others],
+        [packed, from_c, part, from_x],
         (),
         FIRST * flops,
     )
@@ -268,7 +284,8 @@
         specs={i: LEVELS_OF for i in range(1, 1 + GROUP)},
     )
     back = lax.all_to_all(out, ("zl", "c"), 0, 0, tiled=True)
-    return back.transpose(1, 0, 2).reshape(1, TOK, HEADS * HEAD_DIM)
+    (joined,) = call(join_kernel, "join", [((TOK, HEADS * HEAD_DIM), BF16)], [back])
+    return joined[None]
 
 
 def solution(mesh):

time: 103 us -> 102 us (level)
  Pallas kernels: 8.74 us -> 9.96 us
  local copies, waits for them, and re-layouts: 3.89 us -> 2.69 us
  waiting for transfers between devices: 25.8 us -> 24.7 us
    pallas_call x5 -> x7, Pallas kernels: 8.74 us -> 9.96 us  [call(): pl.pallas_call(kernel, out_shape=[jax.ShapeDtypeStruct(shape, dtype) for...]
    ppermute x1, waiting for transfers between devices: 1.05 us -> 0.01 us  [local(): lax.ppermute(same, ('xh', 'xl'), [(i, (i + 1) % X) for i in range(X)])]
  transfers between devices with their start and end apart: 7 -> 7, of which waited for: 4 -> 3; matrix products, arithmetic and copies ran while one was open for 0% -> 0% of each run, Pallas kernels for 5% -> 5%
where the time goes in v4:
time: 102 us; the launch traced here: 100 us
  blocking collectives  33.6 us (33%)
  starting transfers between devices  29 us (28%)
  waiting for transfers between devices  24.7 us (24%)
  Pallas kernels  9.96 us (10%)
  local copies, waits for them, and re-layouts  2.69 us (3%)
    all_to_all x1, blocking collectives, local(): totals = lax.all_to_all(total, 'zh', 0, 0, tiled=True)  18.9 us
    all_to_all x1, waiting for transfers between devices, spread_over(): lax.all_to_all(jnp.broadcast_to(array[None], (size,) + array.shape), axis...  14.7 us
    all_to_all x1, blocking collectives, local(): back = lax.all_to_all(out, ('zl', 'c'), 0, 0, tiled=True)  14.7 us
    ppermute x3, starting transfers between devices, swap(): return lax.ppermute(array, axis, [(i, i ^ bit) for i in range(size)])  10.5 us
    all_to_all x1, starting transfers between devices, spread_over(): lax.all_to_all(jnp.broadcast_to(array[None], (size,) + array.shape), axis...  10.1 us
    pallas_call x7, Pallas kernels, call(): pl.pallas_call(kernel, out_shape=[jax.ShapeDtypeStruct(shape, dtype) for...  9.96 us
    ppermute x1, waiting for transfers between devices, local(): lax.ppermute(same, ('yh', 'yl', 'xh', 'xl'), [(y * X + x, (y - 1) % Y * X...  7.76 us
    ppermute x1, starting transfers between devices, local(): lax.ppermute(same, ('xh', 'xl'), [(i, (i + 1) % X) for i in range(X)])  3.39 us
  transfers between devices with their start and end apart: 7, of which 3 were waited for; matrix products, arithmetic and copies ran while one was open for 0% of the time, Pallas kernels for 5%

profile of v4, /device:TPU:1, one launch (start us, length us, event | category | flops | bytes accessed | tf_op | source)
XLA Modules:
  0.0 100.1 jit_solution(15628579640430281778)
XLA Ops:
  0.0 0.0 copy-start
  0.0 0.9 copy-done
  0.9 0.8 constant_dynamic-slice_fusion
  1.7 0.0 copy-start.1
  1.7 0.0 copy-start.2
  1.7 1.0 broadcast_in_dim.4
  2.7 10.1 %all-to-all-start = ((bf16[8,64,768]{2,1,0:T(8,128)(2,1)}), bf16[8,64,768]{2,1,0:T(8,128)(2,1)}, u32[]{:S(2)}, u32[]{:S(2)}) async-start(bf16[8,64,768]{2,1,0:T(8,128)(2,1)} %broadcast_in_dim.4), calls=%async_computation | async-start | bytes 1572864 | tf_op jit(solution)/shard_map/all_to_all | solution.py:175
  12.8 0.1 pad_add_fusion.place
  12.9 0.0 copy-done.1
  12.9 0.0 copy-done.2
  12.9 1.0 %pack.1.t0 = bf16[272,2048]{1,0:T(8,128)(2,1)S(1)} custom-call(s32[4]{0:T(128)S(1)} %pad_add_fusion.place, bf16[256,2048]{1,0:T(8,128)(2,1)S(1)} %bitcast.11, f32[21,8,256]{2,1,0:T(8,128)S(1)} %bitcast.12), custom_call_target="tpu_custom_call" | custom-call | bytes 8388608 | tf_op jit(solution)/shard_map/pack/pallas_call | solution.py:184
  13.9 4.0 %collective-permute-start.1 = (bf16[272,2048]{1,0:T(8,128)(2,1)S(1)}, bf16[272,2048]{1,0:T(8,128)(2,1)S(1)}, u32[]{:S(2)}, u32[]{:S(2)}) collective-permute-start(bf16[272,2048]{1,0:T(8,128)(2,1)S(1)} %pack.1.t0), channel_id=1, source_target_pairs={{0,2},{2,0},{1,3},{3,1},{4,6},{6,4},{5,7},{7,5},{8,10},{10,8},{9,1... | collective-permute-start | bytes 3342344 | tf_op jit(solution)/shard_map/ppermute | solution.py:171
  18.0 3.1 %collective-permute-start = (bf16[272,2048]{1,0:T(8,128)(2,1)S(1)}, bf16[272,2048]{1,0:T(8,128)(2,1)S(1)}, u32[]{:S(2)}, u32[]{:S(2)}) collective-permute-start(bf16[272,2048]{1,0:T(8,128)(2,1)S(1)} %pack.1.t0), channel_id=1, source_target_pairs={{0,1},{1,0},{2,3},{3,2},{4,5},{5,4},{6,7},{7,6},{8,9},{9,8},{10,11... | collective-permute-start | bytes 3342344 | tf_op jit(solution)/shard_map/ppermute | solution.py:171
  21.1 14.7 %all-to-all-done = bf16[8,64,768]{2,1,0:T(8,128)(2,1)} async-done(((bf16[8,64,768]{2,1,0:T(8,128)(2,1)}), bf16[8,64,768]{2,1,0:T(8,128)(2,1)}, u32[]{:S(2)}, u32[]{:S(2)}) %all-to-all-start) | async-done | bytes 786464 | tf_op jit(solution)/shard_map/all_to_all | solution.py:175
  35.8 1.9 %collective-permute-start.4 = (bf16[512,768]{1,0:T(8,128)(2,1)}, bf16[512,768]{1,0:T(8,128)(2,1)S(1)}, u32[]{:S(2)}, u32[]{:S(2)}) collective-permute-start(bf16[512,768]{1,0:T(8,128)(2,1)} %bitcast.7.w0), channel_id=1, source_target_pairs={{0,496},{16,448},{32,464},{48,480},{64,48},{80,0},{96,16},{112,32}... | collective-permute-start | bytes 2359304 | tf_op jit(solution)/shard_map/ppermute | solution.py:222
  37.7 3.1 %collective-permute-start.3 = (bf16[512,768]{1,0:T(8,128)(2,1)}, bf16[512,768]{1,0:T(8,128)(2,1)S(1)}, u32[]{:S(2)}, u32[]{:S(2)}) collective-permute-start(bf16[512,768]{1,0:T(8,128)(2,1)} %bitcast.7.w0), channel_id=1, source_target_pairs={{0,64},{64,128},{128,192},{192,256},{256,320},{320,384},{384,448},... | collective-permute-start | bytes 2359304 | tf_op jit(solution)/shard_map/ppermute | solution.py:221
  40.8 3.4 %collective-permute-start.5 = (bf16[512,768]{1,0:T(8,128)(2,1)}, bf16[512,768]{1,0:T(8,128)(2,1)S(1)}, u32[]{:S(2)}, u32[]{:S(2)}) collective-permute-start(bf16[512,768]{1,0:T(8,128)(2,1)} %bitcast.7.w0), channel_id=1, source_target_pairs={{0,16},{16,32},{32,48},{48,0},{1,17},{17,33},{33,49},{49,1},{2,18}... | collective-permute-start | bytes 2359304 | tf_op jit(solution)/shard_map/ppermute | solution.py:220
  44.2 0.0 collective-permute-done.1.t2
  44.2 3.4 %collective-permute-start.2 = (bf16[272,2048]{1,0:T(8,128)(2,1)S(1)}, bf16[272,2048]{1,0:T(8,128)(2,1)S(1)}, u32[]{:S(2)}, u32[]{:S(2)}) collective-permute-start(bf16[272,2048]{1,0:T(8,128)(2,1)S(1)} %collective-permute-done.1.t2), channel_id=1, source_target_pairs={{0,1},{1,0},{2,3},{3,2},{4,5},{5,4},{6,7},{7,6},{8,9},{9,8},{10,11... | collective-permute-start | bytes 3342344 | tf_op jit(solution)/shard_map/ppermute | solution.py:171
  47.6 0.0 collective-permute-done.t1
  47.6 1.9 %own_class.1 = (f32[3,256,768]{2,1,0:T(8,128)S(1)}, bf16[512,768]{1,0:T(8,128)(2,1)S(1)}) custom-call(bf16[272,2048]{1,0:T(8,128)(2,1)S(1)} %pack.1.t0, bf16[272,2048]{1,0:T(8,128)(2,1)S(1)} %collective-permute-done.t1, bf16[272,2048]{1,0:T(8,128)(2,1)S(1)} %collective-permute-done.1.t2, bf16[512,768]{1,0:T(8,128)(2,1)} %bitcast.7.w0), custom_call_target="tpu_custom_call" | custom-call | flops 603979776 | bytes 8388608 | tf_op jit(solution)/shard_map/own_class/pallas_call | solution.py:184
  49.5 7.8 %collective-permute-done.4.w3 = bf16[512,768]{1,0:T(8,128)(2,1)S(1)} collective-permute-done((bf16[512,768]{1,0:T(8,128)(2,1)}, bf16[512,768]{1,0:T(8,128)(2,1)S(1)}, u32[]{:S(2)}, u32[]{:S(2)}) %collective-permute-start.4) | collective-permute-done | bytes 786464 | tf_op jit(solution)/shard_map/ppermute | solution.py:222
  57.3 2.2 %collective-permute-done.3.w2 = bf16[512,768]{1,0:T(8,128)(2,1)S(1)} collective-permute-done((bf16[512,768]{1,0:T(8,128)(2,1)}, bf16[512,768]{1,0:T(8,128)(2,1)S(1)}, u32[]{:S(2)}, u32[]{:S(2)}) %collective-permute-start.3) | collective-permute-done | bytes 786464 | tf_op jit(solution)/shard_map/ppermute | solution.py:221
  59.5 1.4 %two_classes.1.part = f32[3,256,768]{2,1,0:T(8,128)S(1)} custom-call(bf16[272,2048]{1,0:T(8,128)(2,1)S(1)} %pack.1.t0, bf16[272,2048]{1,0:T(8,128)(2,1)S(1)} %collective-permute-done.t1, bf16[272,2048]{1,0:T(8,128)(2,1)S(1)} %collective-permute-done.1.t2, f32[3,256,768]{2,1,0:T(8,128)S(1)} %get-tuple-element.23.part, ...), custom_call_target="tpu_custom_call" | custom-call | tf_op jit(solution)/shard_map/two_classes/pallas_call | solution.py:184
  60.9 0.0 collective-permute-done.5.w1
  61.0 0.9 project_here.1
  61.8 0.0 collective-permute-done.2.t3
  61.8 0.0 copy-start.3
  61.8 1.7 %project_there.1 = (bf16[2,256,256]{2,1,0:T(8,128)(2,1)S(1)}, bf16[2,256,256]{2,1,0:T(8,128)(2,1)S(1)}, bf16[2,256,256]{2,1,0:T(8,128)(2,1)S(1)}, bf16[2,2,128,1...) custom-call(bf16[272,2048]{1,0:T(8,128)(2,1)S(1)} %collective-permute-done.1.t2, ...), custom_call_target="tpu_custom_call" | custom-call | flops 1610612736 | bytes 8388608 | tf_op jit(solution)/shard_map/project_there/pallas_call | solution.py:184
  63.5 18.9 %all_to_all.15.totals = bf16[4,2,128,128]{3,2,1,0:T(8,128)(2,1)S(1)} all-to-all(bf16[4,2,128,128]{3,2,1,0:T(8,128)(2,1)S(1)} %get-tuple-element.36), channel_id=1, replica_groups=mesh['yh'=4,'yl'=2,'xh'=2,'xl'=2,'zh'=4,'zl'=2,'c'=2] {'zh'}, dimensions={0} | all-to-all | bytes 524288 | tf_op jit(solution)/shard_map/all_to_all | solution.py:271
  82.4 0.0 copy-done.3
  82.4 2.2 %attend.1 = bf16[4,256,256]{2,1,0:T(8,128)(2,1)S(1)} custom-call(s32[4]{0:T(128)S(1)} %pad_add_fusion.place, bf16[272,2048]{1,0:T(8,128)(2,1)S(1)} %pack.1.t0, bf16[272,2048]{1,0:T(8,128)(2,1)S(1)} %collective-permute-done.t1, bf16[272,2048]{1,0:T(8,128)(2,1)S(1)} %collective-permute-done.1.t2, bf16[272,2048]{1,0:T(8,128)(2,1)S(1)} %collective-permute-done.2.t3, ...), custom_call_target="tpu_custom_call" | custom-call | bytes 8388608 | tf_op jit(solution)/shard_map/attend/pallas_call | solution.py:184
  84.6 14.7 %all_to_all.16.back = bf16[4,256,256]{2,1,0:T(8,128)(2,1)S(1)} all-to-all(bf16[4,256,256]{2,1,0:T(8,128)(2,1)S(1)} %attend.1), channel_id=1, replica_groups=mesh['yh'=4,'yl'=2,'xh'=2,'xl'=2,'zh'=4,'zl'=2,'c'=2] {'zl','c'}, dimensions={0} | all-to-all | bytes 1048576 | tf_op jit(solution)/shard_map/all_to_all | solution.py:286
  99.3 0.9 join.1
  (2 shorter events, 0.0 us)
Async XLA Ops:
  0.0 0.9 copy-start
  1.7 11.2 %copy-start.1 = (bf16[1,256,2048]{2,1,0:T(8,128)(2,1)S(1)}, bf16[1,256,2048]{2,1,0:T(8,128)(2,1)}, u32[]{:S(2)}) copy-start(bf16[1,256,2048]{2,1,0:T(8,128)(2,1)} %param.6) | copy-start | bytes 3145732
  1.7 11.2 %copy-start.2 = (f32[1,8,21,256]{3,1,2,0:T(8,128)S(1)}, f32[1,8,21,256]{3,1,2,0:T(8,128)}, u32[]{:S(2)}) copy-start(f32[1,8,21,256]{3,1,2,0:T(8,128)} %param.7) | copy-start | bytes 516100
  2.7 33.1 %all-to-all-start = ((bf16[8,64,768]{2,1,0:T(8,128)(2,1)}), bf16[8,64,768]{2,1,0:T(8,128)(2,1)}, u32[]{:S(2)}, u32[]{:S(2)}) async-start(bf16[8,64,768]{2,1,0:T(8,128)(2,1)} %broadcast_in_dim.4), calls=%async_computation | async-start | bytes 1572864 | tf_op jit(solution)/shard_map/all_to_all | solution.py:175
  13.9 30.3 %collective-permute-start.1 = (bf16[272,2048]{1,0:T(8,128)(2,1)S(1)}, bf16[272,2048]{1,0:T(8,128)(2,1)S(1)}, u32[]{:S(2)}, u32[]{:S(2)}) collective-permute-start(bf16[272,2048]{1,0:T(8,128)(2,1)S(1)} %pack.1.t0), channel_id=1, source_target_pairs={{0,2},{2,0},{1,3},{3,1},{4,6},{6,4},{5,7},{7,5},{8,10},{10,8},{9,1... | collective-permute-start | bytes 3342344 | tf_op jit(solution)/shard_map/ppermute | solution.py:171
  18.0 29.6 %collective-permute-start = (bf16[272,2048]{1,0:T(8,128)(2,1)S(1)}, bf16[272,2048]{1,0:T(8,128)(2,1)S(1)}, u32[]{:S(2)}, u32[]{:S(2)}) collective-permute-start(bf16[272,2048]{1,0:T(8,128)(2,1)S(1)} %pack.1.t0), channel_id=1, source_target_pairs={{0,1},{1,0},{2,3},{3,2},{4,5},{5,4},{6,7},{7,6},{8,9},{9,8},{10,11... | collective-permute-start | bytes 3342344 | tf_op jit(solution)/shard_map/ppermute | solution.py:171
  35.8 21.5 %collective-permute-start.4 = (bf16[512,768]{1,0:T(8,128)(2,1)}, bf16[512,768]{1,0:T(8,128)(2,1)S(1)}, u32[]{:S(2)}, u32[]{:S(2)}) collective-permute-start(bf16[512,768]{1,0:T(8,128)(2,1)} %bitcast.7.w0), channel_id=1, source_target_pairs={{0,496},{16,448},{32,464},{48,480},{64,48},{80,0},{96,16},{112,32}... | collective-permute-start | bytes 2359304 | tf_op jit(solution)/shard_map/ppermute | solution.py:222
  37.7 21.8 %collective-permute-start.3 = (bf16[512,768]{1,0:T(8,128)(2,1)}, bf16[512,768]{1,0:T(8,128)(2,1)S(1)}, u32[]{:S(2)}, u32[]{:S(2)}) collective-permute-start(bf16[512,768]{1,0:T(8,128)(2,1)} %bitcast.7.w0), channel_id=1, source_target_pairs={{0,64},{64,128},{128,192},{192,256},{256,320},{320,384},{384,448},... | collective-permute-start | bytes 2359304 | tf_op jit(solution)/shard_map/ppermute | solution.py:221
  40.8 20.1 %collective-permute-start.5 = (bf16[512,768]{1,0:T(8,128)(2,1)}, bf16[512,768]{1,0:T(8,128)(2,1)S(1)}, u32[]{:S(2)}, u32[]{:S(2)}) collective-permute-start(bf16[512,768]{1,0:T(8,128)(2,1)} %bitcast.7.w0), channel_id=1, source_target_pairs={{0,16},{16,32},{32,48},{48,0},{1,17},{17,33},{33,49},{49,1},{2,18}... | collective-permute-start | bytes 2359304 | tf_op jit(solution)/shard_map/ppermute | solution.py:220
  44.2 17.6 %collective-permute-start.2 = (bf16[272,2048]{1,0:T(8,128)(2,1)S(1)}, bf16[272,2048]{1,0:T(8,128)(2,1)S(1)}, u32[]{:S(2)}, u32[]{:S(2)}) collective-permute-start(bf16[272,2048]{1,0:T(8,128)(2,1)S(1)} %collective-permute-done.1.t2), channel_id=1, source_target_pairs={{0,1},{1,0},{2,3},{3,2},{4,5},{5,4},{6,7},{7,6},{8,9},{9,8},{10,11... | collective-permute-start | bytes 3342344 | tf_op jit(solution)/shard_map/ppermute | solution.py:171
  61.8 20.6 %copy-start.3 = (f32[1024]{0:T(1024)S(1)}, f32[1024]{0:T(1024)}, u32[]{:S(2)}) copy-start(f32[1024]{0:T(1024)} %param.11) | copy-start | bytes 12292

commit v5 on v4

--- a/solution.py
+++ b/solution.py
@@ -1,3 +1,5 @@
+import functools
+
 import jax
 import jax.numpy as jnp
 from jax import lax
@@ -103,24 +105,24 @@
 
 
 def attend_kernel(
-    place, t0, t1, t2, t3, q0, q1, k0, k1, v0, v1, s0, s1, p0, p1, totals, gain, out, mixed
+    pair, ta, tb, q0, q1, k0, k1, v0, v1, s0, s1, p0, p1, totals, gain, out_a, out_b, mixed
 ):
     queries_in, keys_in, values_in, near_state = (q0, q1), (k0, k1), (v0, v1), (s0, s1)
     pair_state = (p0, p1)
-    role = place[0]
-    group = place[1]
+    role = lax.axis_index(("zl", "c"))
+    group = lax.axis_index("zh")
     half = TOK // 2
     key_pos = lax.broadcasted_iota(jnp.int32, (half, half), 0)
     query_pos = lax.broadcasted_iota(jnp.int32, (half, half), 1)
     xor_pos = jnp.bitwise_xor(key_pos, query_pos)
     causal = key_pos <= query_pos
-    all_tokens = (t0, t1, t2, t3)
+    blocks = (2 * pair, 2 * pair + 1)
 
     def weights_of(j, h):
         start = pl.multiple_of((role * OWN_HEADS + h) * TOK, TOK)
-        return all_tokens[j][:, pl.ds(start, TOK)].astype(F32)
-
-    for j in range(GROUP):
+        return (ta, tb)[j & 1][:, pl.ds(start, TOK)].astype(F32)
+
+    for j in blocks:
         for h in range(OWN_HEADS):
             cols = slice(h * HEAD_DIM, (h + 1) * HEAD_DIM)
             queries = queries_in[j >> 1][j & 1, :, cols]
@@ -128,9 +130,9 @@
             weights = weights_of(j, h)
             first = dot(keys[:half], queries, 1, 1)
             second = dot(keys[half:], queries[half:], 1, 1)
-            mixed[j, h, :half, :half] = gated_quarter(first[:, :half], weights[:, :half], xor_pos, causal, 7)
-            mixed[j, h, :half, half:] = (first[:, half:] * weights[8:9, half:]).astype(BF16)
-            mixed[j, h, half:, half:] = gated_quarter(second, weights[:, half:], xor_pos, causal, 7)
+            mixed[j & 1, h, :half, :half] = gated_quarter(first[:, :half], weights[:, :half], xor_pos, causal, 7)
+            mixed[j & 1, h, :half, half:] = (first[:, half:] * weights[8:9, half:]).astype(BF16)
+            mixed[j & 1, h, half:, half:] = gated_quarter(second, weights[:, half:], xor_pos, causal, 7)
 
     far_use = (jnp.bitwise_and(group, 1).astype(F32), jnp.right_shift(group, 1).astype(F32))
     for h in range(OWN_HEADS):
@@ -138,7 +140,7 @@
         cols = slice(h * HEAD_DIM, (h + 1) * HEAD_DIM)
         far_low = totals[jnp.bitwise_xor(group, 1), h]
         far_high = (totals[0, h].astype(F32) + totals[1, h].astype(F32)).astype(BF16)
-        for j in range(GROUP):
+        for j in blocks:
             block = jnp.bitwise_xor(role, j)
             use = (
                 jnp.bitwise_and(block, 1).astype(F32),
@@ -150,8 +152,8 @@
             )
             remote = dot(states, queries_in[j >> 1][j & 1, :, cols], 1, 1)
             values = values_in[j >> 1][j & 1, cols, :]
-            near_0 = dot(values[:, :half], mixed[j, h, :half, :half], 1, 0)
-            near_1 = dot(values, mixed[j, h, :, half:], 1, 0)
+            near_0 = dot(values[:, :half], mixed[j & 1, h, :half, :half], 1, 0)
+            near_1 = dot(values, mixed[j & 1, h, :, half:], 1, 0)
             summed = jnp.concatenate([near_0, near_1], 1)
             for i in range(4):
                 row = LOW_LEVELS + i
@@ -160,7 +162,7 @@
                 )
             mean_square = jnp.mean(summed * summed, axis=0, keepdims=True)
             normed = (summed * lax.rsqrt(mean_square + 1e-06)).T * gain[head]
-            out[block, :, cols] = normed.astype(BF16)
+            (out_a, out_b)[j & 1][:, cols] = normed.astype(BF16)
 
 
 VMEM = pl.BlockSpec(memory_space=pltpu.VMEM)
@@ -194,9 +196,11 @@
     )(*ins)
 
 
-def join_kernel(back, out):
-    for r in range(GROUP):
-        out[:, r * OWN_COLS : (r + 1) * OWN_COLS] = back[r]
+def join_kernel(p0, p1, p2, p3, out):
+    role = lax.axis_index(("zl", "c"))
+    for j, part in enumerate((p0, p1, p2, p3)):
+        start = pl.multiple_of(jnp.bitwise_xor(role, j) * OWN_COLS, OWN_COLS)
+        out[:, pl.ds(start, OWN_COLS)] = part[...]
 
 
 def local(tokens, level_weights, w_query, w_key, w_value, head_gain):
@@ -269,22 +273,32 @@
         flops,
     )
     totals = lax.all_to_all(total, "zh", 0, 0, tiled=True)
-    (out,) = call(
-        attend_kernel,
-        "attend",
-        [((GROUP, TOK, OWN_COLS), BF16)],
+    gains = head_gain.reshape(HEADS, 1, HEAD_DIM)
+    shared = [array for pair in zip(here, there) for array in pair] + [totals, gains]
+
+    def attend(pair, name):
+        return call(
+            functools.partial(attend_kernel, pair),
+            name,
+            [((TOK, OWN_COLS), BF16)] * 2,
+            [*token_parts[2 * pair : 2 * pair + 2], *shared],
+            [pltpu.VMEM((2, OWN_HEADS, TOK, TOK), BF16)],
+            specs={i: LEVELS_OF for i in (0, 1)},
+        )
+
+    to_z, to_zc = attend(1, "attend_there")
+    kept, to_c = attend(0, "attend_here")
+    (joined,) = call(
+        join_kernel,
+        "join",
+        [((TOK, HEADS * HEAD_DIM), BF16)],
         [
-            place,
-            *token_parts,
-            *[array for pair in zip(here, there) for array in pair],
-            totals,
-            head_gain.reshape(HEADS, 1, HEAD_DIM),
+            kept,
+            swap(to_c, ("zl", "c"), GROUP, 1),
+            swap(to_z, ("zl", "c"), GROUP, 2),
+            swap(to_zc, ("zl", "c"), GROUP, 3),
         ],
-        [pltpu.VMEM((GROUP, OWN_HEADS, TOK, TOK), BF16)],
-        specs={i: LEVELS_OF for i in range(1, 1 + GROUP)},
-    )
-    back = lax.all_to_all(out, ("zl", "c"), 0, 0, tiled=True)
-    (joined,) = call(join_kernel, "join", [((TOK, HEADS * HEAD_DIM), BF16)], [back])
+    )
     return joined[None]
 
 

time: 102 us -> 99.9 us (0.979)
  blocking collectives: 33.6 us -> 18.9 us
  starting transfers between devices: 29 us -> 40.8 us
  waiting for transfers between devices: 24.7 us -> 26 us
    all_to_all x1 -> x0, blocking collectives: 14.7 us -> none  [local(): back = lax.all_to_all(out, ('zl', 'c'), 0, 0, tiled=True)]
    ppermute x3 -> x6, starting transfers between devices: 10.5 us -> 22.3 us  [swap(): return lax.ppermute(array, axis, [(i, i ^ bit) for i in range(size)])]
    ppermute x3 -> x6, waiting for transfers between devices: 0.01 us -> 1.31 us  [swap(): return lax.ppermute(array, axis, [(i, i ^ bit) for i in range(size)])]
    pallas_call x7 -> x8, Pallas kernels: 9.96 us -> 9.67 us  [call(): pl.pallas_call(kernel, out_shape=[jax.ShapeDtypeStruct(shape, dtype) for...]
  transfers between devices with their start and end apart: 7 -> 10, of which waited for: 3 -> 5; matrix products, arithmetic and copies ran while one was open for 0% -> 0% of each run, Pallas kernels for 5% -> 6%
where the time goes in v5:
time: 99.9 us; the launch traced here: 98.4 us
  starting transfers between devices  40.8 us (41%)
  waiting for transfers between devices  26 us (26%)
  blocking collectives  18.9 us (19%)
  Pallas kernels  9.67 us (10%)
  local copies, waits for them, and re-layouts  2.68 us (3%)
    ppermute x6, starting transfers between devices, swap(): return lax.ppermute(array, axis, [(i, i ^ bit) for i in range(size)])  22.3 us
    all_to_all x1, blocking collectives, local(): totals = lax.all_to_all(total, 'zh', 0, 0, tiled=True)  18.9 us
    all_to_all x1, waiting for transfers between devices, spread_over(): lax.all_to_all(jnp.broadcast_to(array[None], (size,) + array.shape), axis...  14.7 us
    all_to_all x1, starting transfers between devices, spread_over(): lax.all_to_all(jnp.broadcast_to(array[None], (size,) + array.shape), axis...  10.1 us
    pallas_call x8, Pallas kernels, call(): pl.pallas_call(kernel, out_shape=[jax.ShapeDtypeStruct(shape, dtype) for...  9.67 us
    ppermute x1, waiting for transfers between devices, local(): lax.ppermute(same, ('yh', 'yl', 'xh', 'xl'), [(y * X + x, (y - 1) % Y * X...  7.76 us
    ppermute x1, starting transfers between devices, local(): lax.ppermute(same, ('xh', 'xl'), [(i, (i + 1) % X) for i in range(X)])  3.39 us
    ppermute x1, starting transfers between devices, local(): lax.ppermute(same, ('yh', 'yl'), [(i, (i + 1) % Y) for i in range(Y)])  3.06 us
  transfers between devices with their start and end apart: 10, of which 5 were waited for; matrix products, arithmetic and copies ran while one was open for 0% of the time, Pallas kernels for 6%

profile of v5, /device:TPU:1, one launch (start us, length us, event | category | flops | bytes accessed | tf_op | source)
XLA Modules:
  0.0 98.4 jit_solution(10315807379365581995)
XLA Ops:
  0.0 0.0 copy-start
  0.0 0.9 copy-done
  0.9 0.8 constant_dynamic-slice_fusion
  1.7 0.0 copy-start.1
  1.7 0.0 copy-start.2
  1.7 1.0 broadcast_in_dim.4
  2.7 10.1 %all-to-all-start = ((bf16[8,64,768]{2,1,0:T(8,128)(2,1)}), bf16[8,64,768]{2,1,0:T(8,128)(2,1)}, u32[]{:S(2)}, u32[]{:S(2)}) async-start(bf16[8,64,768]{2,1,0:T(8,128)(2,1)} %broadcast_in_dim.4), calls=%async_computation | async-start | bytes 1572864 | tf_op jit(solution)/shard_map/all_to_all | solution.py:177
  12.8 0.1 pad_add_fusion.place
  12.9 0.0 copy-done.1
  12.9 0.0 copy-done.2
  12.9 1.0 %pack.1.t0.ta = bf16[272,2048]{1,0:T(8,128)(2,1)S(1)} custom-call(s32[4]{0:T(128)S(1)} %pad_add_fusion.place, bf16[256,2048]{1,0:T(8,128)(2,1)S(1)} %bitcast.11, f32[21,8,256]{2,1,0:T(8,128)S(1)} %bitcast.12), custom_call_target="tpu_custom_call" | custom-call | bytes 8388608 | tf_op jit(solution)/shard_map/pack/pallas_call | solution.py:186
  13.9 4.0 %collective-permute-start.1 = (bf16[272,2048]{1,0:T(8,128)(2,1)S(1)}, bf16[272,2048]{1,0:T(8,128)(2,1)S(1)}, u32[]{:S(2)}, u32[]{:S(2)}) collective-permute-start(bf16[272,2048]{1,0:T(8,128)(2,1)S(1)} %pack.1.t0.ta), channel_id=1, source_target_pairs={{0,2},{2,0},{1,3},{3,1},{4,6},{6,4},{5,7},{7,5},{8,10},{10,8},{9,1... | collective-permute-start | bytes 3342344 | tf_op jit(solution)/shard_map/ppermute | solution.py:173
  17.9 3.1 %collective-permute-start = (bf16[272,2048]{1,0:T(8,128)(2,1)S(1)}, bf16[272,2048]{1,0:T(8,128)(2,1)S(1)}, u32[]{:S(2)}, u32[]{:S(2)}) collective-permute-start(bf16[272,2048]{1,0:T(8,128)(2,1)S(1)} %pack.1.t0.ta), channel_id=1, source_target_pairs={{0,1},{1,0},{2,3},{3,2},{4,5},{5,4},{6,7},{7,6},{8,9},{9,8},{10,11... | collective-permute-start | bytes 3342344 | tf_op jit(solution)/shard_map/ppermute | solution.py:173
  21.1 14.7 %all-to-all-done = bf16[8,64,768]{2,1,0:T(8,128)(2,1)} async-done(((bf16[8,64,768]{2,1,0:T(8,128)(2,1)}), bf16[8,64,768]{2,1,0:T(8,128)(2,1)}, u32[]{:S(2)}, u32[]{:S(2)}) %all-to-all-start) | async-done | bytes 786464 | tf_op jit(solution)/shard_map/all_to_all | solution.py:177
  35.8 1.9 %collective-permute-start.3 = (bf16[512,768]{1,0:T(8,128)(2,1)}, bf16[512,768]{1,0:T(8,128)(2,1)S(1)}, u32[]{:S(2)}, u32[]{:S(2)}) collective-permute-start(bf16[512,768]{1,0:T(8,128)(2,1)} %bitcast.7.w0), channel_id=1, source_target_pairs={{0,496},{16,448},{32,464},{48,480},{64,48},{80,0},{96,16},{112,32}... | collective-permute-start | bytes 2359304 | tf_op jit(solution)/shard_map/ppermute | solution.py:226
  37.7 3.1 %collective-permute-start.2 = (bf16[512,768]{1,0:T(8,128)(2,1)}, bf16[512,768]{1,0:T(8,128)(2,1)S(1)}, u32[]{:S(2)}, u32[]{:S(2)}) collective-permute-start(bf16[512,768]{1,0:T(8,128)(2,1)} %bitcast.7.w0), channel_id=1, source_target_pairs={{0,64},{64,128},{128,192},{192,256},{256,320},{320,384},{384,448},... | collective-permute-start | bytes 2359304 | tf_op jit(solution)/shard_map/ppermute | solution.py:225
  40.8 3.4 %collective-permute-start.4 = (bf16[512,768]{1,0:T(8,128)(2,1)}, bf16[512,768]{1,0:T(8,128)(2,1)S(1)}, u32[]{:S(2)}, u32[]{:S(2)}) collective-permute-start(bf16[512,768]{1,0:T(8,128)(2,1)} %bitcast.7.w0), channel_id=1, source_target_pairs={{0,16},{16,32},{32,48},{48,0},{1,17},{17,33},{33,49},{49,1},{2,18}... | collective-permute-start | bytes 2359304 | tf_op jit(solution)/shard_map/ppermute | solution.py:224
  44.2 0.0 collective-permute-done.1.t2.ta
  44.2 3.4 %collective-permute-start.5 = (bf16[272,2048]{1,0:T(8,128)(2,1)S(1)}, bf16[272,2048]{1,0:T(8,128)(2,1)S(1)}, u32[]{:S(2)}, u32[]{:S(2)}) collective-permute-start(bf16[272,2048]{1,0:T(8,128)(2,1)S(1)} %collective-permute-done.1.t2.ta), channel_id=1, source_target_pairs={{0,1},{1,0},{2,3},{3,2},{4,5},{5,4},{6,7},{7,6},{8,9},{9,8},{10,11... | collective-permute-start | bytes 3342344 | tf_op jit(solution)/shard_map/ppermute | solution.py:173
  47.6 0.0 collective-permute-done.t1.tb
  47.6 1.9 %own_class.1 = (f32[3,256,768]{2,1,0:T(8,128)S(1)}, bf16[512,768]{1,0:T(8,128)(2,1)S(1)}) custom-call(bf16[272,2048]{1,0:T(8,128)(2,1)S(1)} %pack.1.t0.ta, bf16[272,2048]{1,0:T(8,128)(2,1)S(1)} %collective-permute-done.t1.tb, bf16[272,2048]{1,0:T(8,128)(2,1)S(1)} %collective-permute-done.1.t2.ta, bf16[512,768]{1,0:T(8,128)(2,1)} %bitcast.7.w0), custom_call_target="tpu_custom_call" | custom-call | flops 603979776 | bytes 8388608 | tf_op jit(solution)/shard_map/own_class/pallas_call | solution.py:186
  49.5 7.8 %collective-permute-done.3.w3 = bf16[512,768]{1,0:T(8,128)(2,1)S(1)} collective-permute-done((bf16[512,768]{1,0:T(8,128)(2,1)}, bf16[512,768]{1,0:T(8,128)(2,1)S(1)}, u32[]{:S(2)}, u32[]{:S(2)}) %collective-permute-start.3) | collective-permute-done | bytes 786464 | tf_op jit(solution)/shard_map/ppermute | solution.py:226
  57.3 2.2 %collective-permute-done.2.w2 = bf16[512,768]{1,0:T(8,128)(2,1)S(1)} collective-permute-done((bf16[512,768]{1,0:T(8,128)(2,1)}, bf16[512,768]{1,0:T(8,128)(2,1)S(1)}, u32[]{:S(2)}, u32[]{:S(2)}) %collective-permute-start.2) | collective-permute-done | bytes 786464 | tf_op jit(solution)/shard_map/ppermute | solution.py:225
  59.5 1.4 %two_classes.1.part = f32[3,256,768]{2,1,0:T(8,128)S(1)} custom-call(bf16[272,2048]{1,0:T(8,128)(2,1)S(1)} %pack.1.t0.ta, bf16[272,2048]{1,0:T(8,128)(2,1)S(1)} %collective-permute-done.t1.tb, bf16[272,2048]{1,0:T(8,128)(2,1)S(1)} %collective-permute-done.1.t2.ta, f32[3,256,768]{2,1,0:T(8,128)S(1)} %get-tuple-element.27.part, ...), custom_call_target="tpu_custom_call" | custom-call | tf_op jit(solution)/shard_map/two_classes/pallas_call | solution.py:186
  60.9 0.0 collective-permute-done.4.w1
  60.9 0.8 project_here.1
  61.8 0.0 collective-permute-done.5.t3.tb
  61.8 0.0 copy-start.3
  61.8 1.7 %project_there.1 = (bf16[2,256,256]{2,1,0:T(8,128)(2,1)S(1)}, bf16[2,256,256]{2,1,0:T(8,128)(2,1)S(1)}, bf16[2,256,256]{2,1,0:T(8,128)(2,1)S(1)}, bf16[2,2,128,1...) custom-call(bf16[272,2048]{1,0:T(8,128)(2,1)S(1)} %collective-permute-done.1.t2.ta, ...), custom_call_target="tpu_custom_call" | custom-call | flops 1610612736 | bytes 8388608 | tf_op jit(solution)/shard_map/project_there/pallas_call | solution.py:186
  63.5 18.9 %all_to_all.10.totals = bf16[4,2,128,128]{3,2,1,0:T(8,128)(2,1)S(1)} all-to-all(bf16[4,2,128,128]{3,2,1,0:T(8,128)(2,1)S(1)} %get-tuple-element.40), channel_id=1, replica_groups=mesh['yh'=4,'yl'=2,'xh'=2,'xl'=2,'zh'=4,'zl'=2,'c'=2] {'zh'}, dimensions={0} | all-to-all | bytes 524288 | tf_op jit(solution)/shard_map/all_to_all | solution.py:275
  82.4 0.0 copy-done.3
  82.4 1.0 attend_there.1
  83.4 2.5 %collective-permute-start.7 = (bf16[256,256]{1,0:T(8,128)(2,1)S(1)}, bf16[256,256]{1,0:T(8,128)(2,1)S(1)}, u32[]{:S(2)}, u32[]{:S(2)}) collective-permute-start(bf16[256,256]{1,0:T(8,128)(2,1)S(1)} %get-tuple-element.43), channel_id=1, source_target_pairs={{0,2},{1,3},{2,0},{3,1},{4,6},{5,7},{6,4},{7,5},{8,10},{9,11},{10,... | collective-permute-start | bytes 393224 | tf_op jit(solution)/shard_map/ppermute | solution.py:173
  85.8 7.4 %collective-permute-start.8 = (bf16[256,256]{1,0:T(8,128)(2,1)S(1)}, bf16[256,256]{1,0:T(8,128)(2,1)S(1)}, u32[]{:S(2)}, u32[]{:S(2)}) collective-permute-start(bf16[256,256]{1,0:T(8,128)(2,1)S(1)} %get-tuple-element.44), channel_id=1, source_target_pairs={{0,3},{1,2},{2,1},{3,0},{4,7},{5,6},{6,5},{7,4},{8,11},{9,10},{10,... | collective-permute-start | bytes 393224 | tf_op jit(solution)/shard_map/ppermute | solution.py:173
  93.3 1.0 attend_here.1
  94.2 1.9 %collective-permute-start.6 = (bf16[256,256]{1,0:T(8,128)(2,1)S(1)}, bf16[256,256]{1,0:T(8,128)(2,1)S(1)}, u32[]{:S(2)}, u32[]{:S(2)}) collective-permute-start(bf16[256,256]{1,0:T(8,128)(2,1)S(1)} %get-tuple-element.42), channel_id=1, source_target_pairs={{0,1},{1,0},{2,3},{3,2},{4,5},{5,4},{6,7},{7,6},{8,9},{9,8},{10,11... | collective-permute-start | bytes 393224 | tf_op jit(solution)/shard_map/ppermute | solution.py:173
  96.2 0.0 collective-permute-done.7.p2
  96.2 1.2 %collective-permute-done.8.p3 = bf16[256,256]{1,0:T(8,128)(2,1)S(1)} collective-permute-done((bf16[256,256]{1,0:T(8,128)(2,1)S(1)}, bf16[256,256]{1,0:T(8,128)(2,1)S(1)}, u32[]{:S(2)}, u32[]{:S(2)}) %collective-permute-start.8) | collective-permute-done | bytes 131104 | tf_op jit(solution)/shard_map/ppermute | solution.py:173
  97.4 0.1 collective-permute-done.6.p1
  97.5 0.9 join.1
  (2 shorter events, 0.0 us)
Async XLA Ops:
  0.0 0.9 copy-start
  1.7 11.2 %copy-start.1 = (bf16[1,256,2048]{2,1,0:T(8,128)(2,1)S(1)}, bf16[1,256,2048]{2,1,0:T(8,128)(2,1)}, u32[]{:S(2)}) copy-start(bf16[1,256,2048]{2,1,0:T(8,128)(2,1)} %param.6) | copy-start | bytes 3145732
  1.7 11.2 %copy-start.2 = (f32[1,8,21,256]{3,1,2,0:T(8,128)S(1)}, f32[1,8,21,256]{3,1,2,0:T(8,128)}, u32[]{:S(2)}) copy-start(f32[1,8,21,256]{3,1,2,0:T(8,128)} %param.7) | copy-start | bytes 516100
  2.7 33.1 %all-to-all-start = ((bf16[8,64,768]{2,1,0:T(8,128)(2,1)}), bf16[8,64,768]{2,1,0:T(8,128)(2,1)}, u32[]{:S(2)}, u32[]{:S(2)}) async-start(bf16[8,64,768]{2,1,0:T(8,128)(2,1)} %broadcast_in_dim.4), calls=%async_computation | async-start | bytes 1572864 | tf_op jit(solution)/shard_map/all_to_all | solution.py:177
  13.9 30.3 %collective-permute-start.1 = (bf16[272,2048]{1,0:T(8,128)(2,1)S(1)}, bf16[272,2048]{1,0:T(8,128)(2,1)S(1)}, u32[]{:S(2)}, u32[]{:S(2)}) collective-permute-start(bf16[272,2048]{1,0:T(8,128)(2,1)S(1)} %pack.1.t0.ta), channel_id=1, source_target_pairs={{0,2},{2,0},{1,3},{3,1},{4,6},{6,4},{5,7},{7,5},{8,10},{10,8},{9,1... | collective-permute-start | bytes 3342344 | tf_op jit(solution)/shard_map/ppermute | solution.py:173
  17.9 29.6 %collective-permute-start = (bf16[272,2048]{1,0:T(8,128)(2,1)S(1)}, bf16[272,2048]{1,0:T(8,128)(2,1)S(1)}, u32[]{:S(2)}, u32[]{:S(2)}) collective-permute-start(bf16[272,2048]{1,0:T(8,128)(2,1)S(1)} %pack.1.t0.ta), channel_id=1, source_target_pairs={{0,1},{1,0},{2,3},{3,2},{4,5},{5,4},{6,7},{7,6},{8,9},{9,8},{10,11... | collective-permute-start | bytes 3342344 | tf_op jit(solution)/shard_map/ppermute | solution.py:173
  35.8 21.5 %collective-permute-start.3 = (bf16[512,768]{1,0:T(8,128)(2,1)}, bf16[512,768]{1,0:T(8,128)(2,1)S(1)}, u32[]{:S(2)}, u32[]{:S(2)}) collective-permute-start(bf16[512,768]{1,0:T(8,128)(2,1)} %bitcast.7.w0), channel_id=1, source_target_pairs={{0,496},{16,448},{32,464},{48,480},{64,48},{80,0},{96,16},{112,32}... | collective-permute-start | bytes 2359304 | tf_op jit(solution)/shard_map/ppermute | solution.py:226
  37.7 21.8 %collective-permute-start.2 = (bf16[512,768]{1,0:T(8,128)(2,1)}, bf16[512,768]{1,0:T(8,128)(2,1)S(1)}, u32[]{:S(2)}, u32[]{:S(2)}) collective-permute-start(bf16[512,768]{1,0:T(8,128)(2,1)} %bitcast.7.w0), channel_id=1, source_target_pairs={{0,64},{64,128},{128,192},{192,256},{256,320},{320,384},{384,448},... | collective-permute-start | bytes 2359304 | tf_op jit(solution)/shard_map/ppermute | solution.py:225
  40.8 20.1 %collective-permute-start.4 = (bf16[512,768]{1,0:T(8,128)(2,1)}, bf16[512,768]{1,0:T(8,128)(2,1)S(1)}, u32[]{:S(2)}, u32[]{:S(2)}) collective-permute-start(bf16[512,768]{1,0:T(8,128)(2,1)} %bitcast.7.w0), channel_id=1, source_target_pairs={{0,16},{16,32},{32,48},{48,0},{1,17},{17,33},{33,49},{49,1},{2,18}... | collective-permute-start | bytes 2359304 | tf_op jit(solution)/shard_map/ppermute | solution.py:224
  44.2 17.6 %collective-permute-start.5 = (bf16[272,2048]{1,0:T(8,128)(2,1)S(1)}, bf16[272,2048]{1,0:T(8,128)(2,1)S(1)}, u32[]{:S(2)}, u32[]{:S(2)}) collective-permute-start(bf16[272,2048]{1,0:T(8,128)(2,1)S(1)} %collective-permute-done.1.t2.ta), channel_id=1, source_target_pairs={{0,1},{1,0},{2,3},{3,2},{4,5},{5,4},{6,7},{7,6},{8,9},{9,8},{10,11... | collective-permute-start | bytes 3342344 | tf_op jit(solution)/shard_map/ppermute | solution.py:173
  61.8 20.6 %copy-start.3 = (f32[1024]{0:T(1024)S(1)}, f32[1024]{0:T(1024)}, u32[]{:S(2)}) copy-start(f32[1024]{0:T(1024)} %param.11) | copy-start | bytes 12292
  83.4 12.8 %collective-permute-start.7 = (bf16[256,256]{1,0:T(8,128)(2,1)S(1)}, bf16[256,256]{1,0:T(8,128)(2,1)S(1)}, u32[]{:S(2)}, u32[]{:S(2)}) collective-permute-start(bf16[256,256]{1,0:T(8,128)(2,1)S(1)} %get-tuple-element.43), channel_id=1, source_target_pairs={{0,2},{1,3},{2,0},{3,1},{4,6},{5,7},{6,4},{7,5},{8,10},{9,11},{10,... | collective-permute-start | bytes 393224 | tf_op jit(solution)/shard_map/ppermute | solution.py:173
  85.8 11.6 %collective-permute-start.8 = (bf16[256,256]{1,0:T(8,128)(2,1)S(1)}, bf16[256,256]{1,0:T(8,128)(2,1)S(1)}, u32[]{:S(2)}, u32[]{:S(2)}) collective-permute-start(bf16[256,256]{1,0:T(8,128)(2,1)S(1)} %get-tuple-element.44), channel_id=1, source_target_pairs={{0,3},{1,2},{2,1},{3,0},{4,7},{5,6},{6,5},{7,4},{8,11},{9,10},{10,... | collective-permute-start | bytes 393224 | tf_op jit(solution)/shard_map/ppermute | solution.py:173
  94.2 3.2 %collective-permute-start.6 = (bf16[256,256]{1,0:T(8,128)(2,1)S(1)}, bf16[256,256]{1,0:T(8,128)(2,1)S(1)}, u32[]{:S(2)}, u32[]{:S(2)}) collective-permute-start(bf16[256,256]{1,0:T(8,128)(2,1)S(1)} %get-tuple-element.42), channel_id=1, source_target_pairs={{0,1},{1,0},{2,3},{3,2},{4,5},{5,4},{6,7},{7,6},{8,9},{9,8},{10,11... | collective-permute-start | bytes 393224 | tf_op jit(solution)/shard_map/ppermute | solution.py:173

commit v6 on v5

--- a/solution.py
+++ b/solution.py
@@ -28,10 +28,18 @@
     return lax.dot_general(a, b, (((ca,), (cb,)), ((), ())), preferred_element_type=F32)
 
 
-def pack_kernel(place, tokens, level_weights, packed):
+def spread_kernel(w_key, w_value, w_query, out):
+    start = pl.multiple_of(lax.axis_index(("zl", "c")) * OWN_COLS, OWN_COLS)
+    for i, matrix in enumerate((w_key, w_value, w_query)):
+        here = matrix[:, pl.ds(start, OWN_COLS)]
+        for copy in range(Y * X // 4):
+            out[copy, :, i * OWN_COLS : (i + 1) * OWN_COLS] = here
+
+
+def pack_kernel(tokens, level_weights, packed):
     for a in range(2):
         for b in range(2):
-            apart = 2 * jnp.bitwise_xor(place[2], a) + jnp.bitwise_xor(place[3], b)
+            apart = 2 * jnp.bitwise_xor(lax.axis_index("yl"), a) + jnp.bitwise_xor(lax.axis_index("xl"), b)
             for yh in range(Y // 2):
                 pieces = []
                 for xh in range(X // 2):
@@ -173,12 +181,6 @@
     return lax.ppermute(array, axis, [(i, i ^ bit) for i in range(size)])
 
 
-def spread_over(array, axis, size):
-    return lax.all_to_all(
-        jnp.broadcast_to(array[None], (size,) + array.shape), axis, 0, 0, tiled=True
-    )
-
-
 LEVELS_OF = pl.BlockSpec((PAD_ROWS, Y * X * SHARD), lambda i: (TOK // PAD_ROWS, 0))
 
 
@@ -204,23 +206,23 @@
 
 
 def local(tokens, level_weights, w_query, w_key, w_value, head_gain):
-    role = lax.axis_index(("zl", "c"))
-    group = lax.axis_index("zh")
-    place = jnp.stack([role, group, lax.axis_index("yl"), lax.axis_index("xl")]).astype(jnp.int32)
-    def own(matrix):
-        return lax.dynamic_slice_in_dim(matrix, role * OWN_COLS, OWN_COLS, 1)
-
-    columns = jnp.concatenate([own(w_key), own(w_value), own(w_query)], 1)
-    columns, tokens_later = lax.optimization_barrier((columns, tokens))
+    (spread,) = call(
+        spread_kernel,
+        "spread",
+        [((Y * X // 4, SHARD, 3 * OWN_COLS), BF16)],
+        [w_key, w_value, w_query],
+        traffic=0,
+    )
+    spread, tokens_later = lax.optimization_barrier((spread, tokens))
     (packed,) = call(
         pack_kernel,
         "pack",
         [((TOK + PAD_ROWS, Y * X * SHARD), BF16)],
-        [place, tokens_later[0], level_weights[0].transpose(1, 0, 2)],
+        [tokens_later[0], level_weights[0].transpose(1, 0, 2)],
     )
     from_z = swap(packed, "zl", 2, 1)
     from_c = swap(packed, "c", 2, 1)
-    same = spread_over(columns, ("yh", "xh"), Y * X // 4).reshape(CLASS_ROWS, 3 * OWN_COLS)
+    same = lax.all_to_all(spread, ("yh", "xh"), 0, 0, tiled=True).reshape(CLASS_ROWS, 3 * OWN_COLS)
     from_x = lax.ppermute(same, ("xh", "xl"), [(i, (i + 1) % X) for i in range(X)])
     from_y = lax.ppermute(same, ("yh", "yl"), [(i, (i + 1) % Y) for i in range(Y)])
     from_yx = lax.ppermute(

time: 99.9 us -> 101 us (1.011)
    unnamed x8 -> x12, local copies, waits for them, and re-layouts: 0.92 us -> 2.82 us
    pallas_call x8 -> x9, Pallas kernels: 9.67 us -> 10.1 us  [call(): pl.pallas_call(kernel, out_shape=[jax.ShapeDtypeStruct(shape, dtype) for...]
where the time goes in v6:
time: 101 us; the launch traced here: 99.4 us
  starting transfers between devices  40.8 us (40%)
  waiting for transfers between devices  26.6 us (26%)
  blocking collectives  18.9 us (19%)
  Pallas kernels  10.1 us (10%)
  local copies, waits for them, and re-layouts  2.82 us (3%)
    ppermute x6, starting transfers between devices, swap(): return lax.ppermute(array, axis, [(i, i ^ bit) for i in range(size)])  22.3 us
    all_to_all x1, blocking collectives, local(): totals = lax.all_to_all(total, 'zh', 0, 0, tiled=True)  18.9 us
    all_to_all x1, waiting for transfers between devices, local(): lax.all_to_all(spread, ('yh', 'xh'), 0, 0, tiled=True)  15.3 us
    all_to_all x1, starting transfers between devices, local(): lax.all_to_all(spread, ('yh', 'xh'), 0, 0, tiled=True)  10.1 us
    pallas_call x9, Pallas kernels, call(): pl.pallas_call(kernel, out_shape=[jax.ShapeDtypeStruct(shape, dtype) for...  10.1 us
    ppermute x1, waiting for transfers between devices, local(): lax.ppermute(same, ('yh', 'yl', 'xh', 'xl'), [(y * X + x, (y - 1) % Y * X...  7.76 us
    ppermute x1, starting transfers between devices, local(): lax.ppermute(same, ('xh', 'xl'), [(i, (i + 1) % X) for i in range(X)])  3.39 us
    ppermute x1, starting transfers between devices, local(): lax.ppermute(same, ('yh', 'yl'), [(i, (i + 1) % Y) for i in range(Y)])  3.06 us
  transfers between devices with their start and end apart: 10, of which 5 were waited for; matrix products, arithmetic and copies ran while one was open for 0% of the time, Pallas kernels for 6%

profile of v6, /device:TPU:1, one launch (start us, length us, event | category | flops | bytes accessed | tf_op | source)
XLA Modules:
  0.0 99.4 jit_solution(3012685229783744860)
XLA Ops:
  0.0 0.0 copy-start
  0.0 0.0 copy-start.1
  0.0 0.0 copy-start.2
  0.0 1.0 %copy-done.2 = bf16[64,1024]{1,0:T(8,128)(2,1)S(1)} copy-done((bf16[64,1024]{1,0:T(8,128)(2,1)S(1)}, bf16[64,1024]{1,0:T(8,128)(2,1)}, u32[]{:S(2)}) %copy-start.2) | copy-done | bytes 131096
  1.0 0.0 copy-start.3
  1.0 0.9 copy-done.3
  1.9 0.0 copy-start.4
  1.9 0.9 copy-done.4
  2.8 1.0 spread.1
  3.8 10.1 %all-to-all-start = ((bf16[8,64,768]{2,1,0:T(8,128)(2,1)}), bf16[8,64,768]{2,1,0:T(8,128)(2,1)}, u32[]{:S(2)}, u32[]{:S(2)}) async-start(bf16[8,64,768]{2,1,0:T(8,128)(2,1)} %spread.1), calls=%async_computation | async-start | bytes 1572864 | tf_op jit(solution)/shard_map/all_to_all | solution.py:225
  13.9 0.0 copy-done
  13.9 0.0 copy-done.1
  13.9 0.5 pack.1.t0.ta
  14.4 4.0 %collective-permute-start.1 = (bf16[272,2048]{1,0:T(8,128)(2,1)S(1)}, bf16[272,2048]{1,0:T(8,128)(2,1)S(1)}, u32[]{:S(2)}, u32[]{:S(2)}) collective-permute-start(bf16[272,2048]{1,0:T(8,128)(2,1)S(1)} %pack.1.t0.ta), channel_id=1, source_target_pairs={{0,2},{2,0},{1,3},{3,1},{4,6},{6,4},{5,7},{7,5},{8,10},{10,8},{9,1... | collective-permute-start | bytes 3342344 | tf_op jit(solution)/shard_map/ppermute | solution.py:181
  18.4 3.1 %collective-permute-start = (bf16[272,2048]{1,0:T(8,128)(2,1)S(1)}, bf16[272,2048]{1,0:T(8,128)(2,1)S(1)}, u32[]{:S(2)}, u32[]{:S(2)}) collective-permute-start(bf16[272,2048]{1,0:T(8,128)(2,1)S(1)} %pack.1.t0.ta), channel_id=1, source_target_pairs={{0,1},{1,0},{2,3},{3,2},{4,5},{5,4},{6,7},{7,6},{8,9},{9,8},{10,11... | collective-permute-start | bytes 3342344 | tf_op jit(solution)/shard_map/ppermute | solution.py:181
  21.6 15.3 %all-to-all-done = bf16[8,64,768]{2,1,0:T(8,128)(2,1)} async-done(((bf16[8,64,768]{2,1,0:T(8,128)(2,1)}), bf16[8,64,768]{2,1,0:T(8,128)(2,1)}, u32[]{:S(2)}, u32[]{:S(2)}) %all-to-all-start) | async-done | bytes 786464 | tf_op jit(solution)/shard_map/all_to_all | solution.py:225
  36.9 1.9 %collective-permute-start.3 = (bf16[512,768]{1,0:T(8,128)(2,1)}, bf16[512,768]{1,0:T(8,128)(2,1)S(1)}, u32[]{:S(2)}, u32[]{:S(2)}) collective-permute-start(bf16[512,768]{1,0:T(8,128)(2,1)} %bitcast.3.w0), channel_id=1, source_target_pairs={{0,496},{16,448},{32,464},{48,480},{64,48},{80,0},{96,16},{112,32}... | collective-permute-start | bytes 2359304 | tf_op jit(solution)/shard_map/ppermute | solution.py:228
  38.8 3.1 %collective-permute-start.2 = (bf16[512,768]{1,0:T(8,128)(2,1)}, bf16[512,768]{1,0:T(8,128)(2,1)S(1)}, u32[]{:S(2)}, u32[]{:S(2)}) collective-permute-start(bf16[512,768]{1,0:T(8,128)(2,1)} %bitcast.3.w0), channel_id=1, source_target_pairs={{0,64},{64,128},{128,192},{192,256},{256,320},{320,384},{384,448},... | collective-permute-start | bytes 2359304 | tf_op jit(solution)/shard_map/ppermute | solution.py:227
  41.9 3.4 %collective-permute-start.4 = (bf16[512,768]{1,0:T(8,128)(2,1)}, bf16[512,768]{1,0:T(8,128)(2,1)S(1)}, u32[]{:S(2)}, u32[]{:S(2)}) collective-permute-start(bf16[512,768]{1,0:T(8,128)(2,1)} %bitcast.3.w0), channel_id=1, source_target_pairs={{0,16},{16,32},{32,48},{48,0},{1,17},{17,33},{33,49},{49,1},{2,18}... | collective-permute-start | bytes 2359304 | tf_op jit(solution)/shard_map/ppermute | solution.py:226
  45.3 0.0 collective-permute-done.1.t2.ta
  45.3 3.4 %collective-permute-start.5 = (bf16[272,2048]{1,0:T(8,128)(2,1)S(1)}, bf16[272,2048]{1,0:T(8,128)(2,1)S(1)}, u32[]{:S(2)}, u32[]{:S(2)}) collective-permute-start(bf16[272,2048]{1,0:T(8,128)(2,1)S(1)} %collective-permute-done.1.t2.ta), channel_id=1, source_target_pairs={{0,1},{1,0},{2,3},{3,2},{4,5},{5,4},{6,7},{7,6},{8,9},{9,8},{10,11... | collective-permute-start | bytes 3342344 | tf_op jit(solution)/shard_map/ppermute | solution.py:181
  48.7 0.0 collective-permute-done.t1.tb
  48.7 1.9 %own_class.1 = (f32[3,256,768]{2,1,0:T(8,128)S(1)}, bf16[512,768]{1,0:T(8,128)(2,1)S(1)}) custom-call(bf16[272,2048]{1,0:T(8,128)(2,1)S(1)} %pack.1.t0.ta, bf16[272,2048]{1,0:T(8,128)(2,1)S(1)} %collective-permute-done.t1.tb, bf16[272,2048]{1,0:T(8,128)(2,1)S(1)} %collective-permute-done.1.t2.ta, bf16[512,768]{1,0:T(8,128)(2,1)} %bitcast.3.w0), custom_call_target="tpu_custom_call" | custom-call | flops 603979776 | bytes 8388608 | tf_op jit(solution)/shard_map/own_class/pallas_call | solution.py:188
  50.6 7.8 %collective-permute-done.3.w3 = bf16[512,768]{1,0:T(8,128)(2,1)S(1)} collective-permute-done((bf16[512,768]{1,0:T(8,128)(2,1)}, bf16[512,768]{1,0:T(8,128)(2,1)S(1)}, u32[]{:S(2)}, u32[]{:S(2)}) %collective-permute-start.3) | collective-permute-done | bytes 786464 | tf_op jit(solution)/shard_map/ppermute | solution.py:228
  58.4 2.2 %collective-permute-done.2.w2 = bf16[512,768]{1,0:T(8,128)(2,1)S(1)} collective-permute-done((bf16[512,768]{1,0:T(8,128)(2,1)}, bf16[512,768]{1,0:T(8,128)(2,1)S(1)}, u32[]{:S(2)}, u32[]{:S(2)}) %collective-permute-start.2) | collective-permute-done | bytes 786464 | tf_op jit(solution)/shard_map/ppermute | solution.py:227
  60.6 1.4 %two_classes.1.part = f32[3,256,768]{2,1,0:T(8,128)S(1)} custom-call(bf16[272,2048]{1,0:T(8,128)(2,1)S(1)} %pack.1.t0.ta, bf16[272,2048]{1,0:T(8,128)(2,1)S(1)} %collective-permute-done.t1.tb, bf16[272,2048]{1,0:T(8,128)(2,1)S(1)} %collective-permute-done.1.t2.ta, f32[3,256,768]{2,1,0:T(8,128)S(1)} %get-tuple-element.27.part, ...), custom_call_target="tpu_custom_call" | custom-call | tf_op jit(solution)/shard_map/two_classes/pallas_call | solution.py:188
  62.0 0.0 collective-permute-done.4.w1
  62.0 0.8 project_here.1
  62.9 0.0 collective-permute-done.5.t3.tb
  62.9 0.0 copy-start.5
  62.9 1.7 %project_there.1 = (bf16[2,256,256]{2,1,0:T(8,128)(2,1)S(1)}, bf16[2,256,256]{2,1,0:T(8,128)(2,1)S(1)}, bf16[2,256,256]{2,1,0:T(8,128)(2,1)S(1)}, bf16[2,2,128,1...) custom-call(bf16[272,2048]{1,0:T(8,128)(2,1)S(1)} %collective-permute-done.1.t2.ta, ...), custom_call_target="tpu_custom_call" | custom-call | flops 1610612736 | bytes 8388608 | tf_op jit(solution)/shard_map/project_there/pallas_call | solution.py:188
  64.6 18.9 %all_to_all.10.totals = bf16[4,2,128,128]{3,2,1,0:T(8,128)(2,1)S(1)} all-to-all(bf16[4,2,128,128]{3,2,1,0:T(8,128)(2,1)S(1)} %get-tuple-element.40), channel_id=1, replica_groups=mesh['yh'=4,'yl'=2,'xh'=2,'xl'=2,'zh'=4,'zl'=2,'c'=2] {'zh'}, dimensions={0} | all-to-all | bytes 524288 | tf_op jit(solution)/shard_map/all_to_all | solution.py:277
  83.5 0.0 copy-done.5
  83.5 1.0 attend_there.1
  84.4 2.5 %collective-permute-start.7 = (bf16[256,256]{1,0:T(8,128)(2,1)S(1)}, bf16[256,256]{1,0:T(8,128)(2,1)S(1)}, u32[]{:S(2)}, u32[]{:S(2)}) collective-permute-start(bf16[256,256]{1,0:T(8,128)(2,1)S(1)} %get-tuple-element.43), channel_id=1, source_target_pairs={{0,2},{1,3},{2,0},{3,1},{4,6},{5,7},{6,4},{7,5},{8,10},{9,11},{10,... | collective-permute-start | bytes 393224 | tf_op jit(solution)/shard_map/ppermute | solution.py:181
  86.9 7.4 %collective-permute-start.8 = (bf16[256,256]{1,0:T(8,128)(2,1)S(1)}, bf16[256,256]{1,0:T(8,128)(2,1)S(1)}, u32[]{:S(2)}, u32[]{:S(2)}) collective-permute-start(bf16[256,256]{1,0:T(8,128)(2,1)S(1)} %get-tuple-element.44), channel_id=1, source_target_pairs={{0,3},{1,2},{2,1},{3,0},{4,7},{5,6},{6,5},{7,4},{8,11},{9,10},{10,... | collective-permute-start | bytes 393224 | tf_op jit(solution)/shard_map/ppermute | solution.py:181
  94.4 1.0 attend_here.1
  95.3 1.9 %collective-permute-start.6 = (bf16[256,256]{1,0:T(8,128)(2,1)S(1)}, bf16[256,256]{1,0:T(8,128)(2,1)S(1)}, u32[]{:S(2)}, u32[]{:S(2)}) collective-permute-start(bf16[256,256]{1,0:T(8,128)(2,1)S(1)} %get-tuple-element.42), channel_id=1, source_target_pairs={{0,1},{1,0},{2,3},{3,2},{4,5},{5,4},{6,7},{7,6},{8,9},{9,8},{10,11... | collective-permute-start | bytes 393224 | tf_op jit(solution)/shard_map/ppermute | solution.py:181
  97.3 0.0 collective-permute-done.7.p2
  97.3 1.2 %collective-permute-done.8.p3 = bf16[256,256]{1,0:T(8,128)(2,1)S(1)} collective-permute-done((bf16[256,256]{1,0:T(8,128)(2,1)S(1)}, bf16[256,256]{1,0:T(8,128)(2,1)S(1)}, u32[]{:S(2)}, u32[]{:S(2)}) %collective-permute-start.8) | collective-permute-done | bytes 131104 | tf_op jit(solution)/shard_map/ppermute | solution.py:181
  98.5 0.1 collective-permute-done.6.p1
  98.6 0.9 join.1
Async XLA Ops:
  0.0 13.9 %copy-start = (bf16[1,256,2048]{2,1,0:T(8,128)(2,1)S(1)}, bf16[1,256,2048]{2,1,0:T(8,128)(2,1)}, u32[]{:S(2)}) copy-start(bf16[1,256,2048]{2,1,0:T(8,128)(2,1)} %param.6) | copy-start | bytes 3145732
  0.0 13.9 %copy-start.1 = (f32[1,8,21,256]{3,1,2,0:T(8,128)S(1)}, f32[1,8,21,256]{3,1,2,0:T(8,128)}, u32[]{:S(2)}) copy-start(f32[1,8,21,256]{3,1,2,0:T(8,128)} %param.7) | copy-start | bytes 516100
  0.0 1.0 %copy-start.2 = (bf16[64,1024]{1,0:T(8,128)(2,1)S(1)}, bf16[64,1024]{1,0:T(8,128)(2,1)}, u32[]{:S(2)}) copy-start(bf16[64,1024]{1,0:T(8,128)(2,1)} %w_key.1) | copy-start | bytes 393220
  1.0 0.9 copy-start.3
  1.9 0.9 copy-start.4
  3.8 33.1 %all-to-all-start = ((bf16[8,64,768]{2,1,0:T(8,128)(2,1)}), bf16[8,64,768]{2,1,0:T(8,128)(2,1)}, u32[]{:S(2)}, u32[]{:S(2)}) async-start(bf16[8,64,768]{2,1,0:T(8,128)(2,1)} %spread.1), calls=%async_computation | async-start | bytes 1572864 | tf_op jit(solution)/shard_map/all_to_all | solution.py:225
  14.4 30.9 %collective-permute-start.1 = (bf16[272,2048]{1,0:T(8,128)(2,1)S(1)}, bf16[272,2048]{1,0:T(8,128)(2,1)S(1)}, u32[]{:S(2)}, u32[]{:S(2)}) collective-permute-start(bf16[272,2048]{1,0:T(8,128)(2,1)S(1)} %pack.1.t0.ta), channel_id=1, source_target_pairs={{0,2},{2,0},{1,3},{3,1},{4,6},{6,4},{5,7},{7,5},{8,10},{10,8},{9,1... | collective-permute-start | bytes 3342344 | tf_op jit(solution)/shard_map/ppermute | solution.py:181
  18.4 30.2 %collective-permute-start = (bf16[272,2048]{1,0:T(8,128)(2,1)S(1)}, bf16[272,2048]{1,0:T(8,128)(2,1)S(1)}, u32[]{:S(2)}, u32[]{:S(2)}) collective-permute-start(bf16[272,2048]{1,0:T(8,128)(2,1)S(1)} %pack.1.t0.ta), channel_id=1, source_target_pairs={{0,1},{1,0},{2,3},{3,2},{4,5},{5,4},{6,7},{7,6},{8,9},{9,8},{10,11... | collective-permute-start | bytes 3342344 | tf_op jit(solution)/shard_map/ppermute | solution.py:181
  36.9 21.5 %collective-permute-start.3 = (bf16[512,768]{1,0:T(8,128)(2,1)}, bf16[512,768]{1,0:T(8,128)(2,1)S(1)}, u32[]{:S(2)}, u32[]{:S(2)}) collective-permute-start(bf16[512,768]{1,0:T(8,128)(2,1)} %bitcast.3.w0), channel_id=1, source_target_pairs={{0,496},{16,448},{32,464},{48,480},{64,48},{80,0},{96,16},{112,32}... | collective-permute-start | bytes 2359304 | tf_op jit(solution)/shard_map/ppermute | solution.py:228
  38.8 21.8 %collective-permute-start.2 = (bf16[512,768]{1,0:T(8,128)(2,1)}, bf16[512,768]{1,0:T(8,128)(2,1)S(1)}, u32[]{:S(2)}, u32[]{:S(2)}) collective-permute-start(bf16[512,768]{1,0:T(8,128)(2,1)} %bitcast.3.w0), channel_id=1, source_target_pairs={{0,64},{64,128},{128,192},{192,256},{256,320},{320,384},{384,448},... | collective-permute-start | bytes 2359304 | tf_op jit(solution)/shard_map/ppermute | solution.py:227
  41.9 20.1 %collective-permute-start.4 = (bf16[512,768]{1,0:T(8,128)(2,1)}, bf16[512,768]{1,0:T(8,128)(2,1)S(1)}, u32[]{:S(2)}, u32[]{:S(2)}) collective-permute-start(bf16[512,768]{1,0:T(8,128)(2,1)} %bitcast.3.w0), channel_id=1, source_target_pairs={{0,16},{16,32},{32,48},{48,0},{1,17},{17,33},{33,49},{49,1},{2,18}... | collective-permute-start | bytes 2359304 | tf_op jit(solution)/shard_map/ppermute | solution.py:226
  45.3 17.6 %collective-permute-start.5 = (bf16[272,2048]{1,0:T(8,128)(2,1)S(1)}, bf16[272,2048]{1,0:T(8,128)(2,1)S(1)}, u32[]{:S(2)}, u32[]{:S(2)}) collective-permute-start(bf16[272,2048]{1,0:T(8,128)(2,1)S(1)} %collective-permute-done.1.t2.ta), channel_id=1, source_target_pairs={{0,1},{1,0},{2,3},{3,2},{4,5},{5,4},{6,7},{7,6},{8,9},{9,8},{10,11... | collective-permute-start | bytes 3342344 | tf_op jit(solution)/shard_map/ppermute | solution.py:181
  62.9 20.6 %copy-start.5 = (f32[1024]{0:T(1024)S(1)}, f32[1024]{0:T(1024)}, u32[]{:S(2)}) copy-start(f32[1024]{0:T(1024)} %param.11) | copy-start | bytes 12292
  84.4 12.8 %collective-permute-start.7 = (bf16[256,256]{1,0:T(8,128)(2,1)S(1)}, bf16[256,256]{1,0:T(8,128)(2,1)S(1)}, u32[]{:S(2)}, u32[]{:S(2)}) collective-permute-start(bf16[256,256]{1,0:T(8,128)(2,1)S(1)} %get-tuple-element.43), channel_id=1, source_target_pairs={{0,2},{1,3},{2,0},{3,1},{4,6},{5,7},{6,4},{7,5},{8,10},{9,11},{10,... | collective-permute-start | bytes 393224 | tf_op jit(solution)/shard_map/ppermute | solution.py:181
  86.9 11.6 %collective-permute-start.8 = (bf16[256,256]{1,0:T(8,128)(2,1)S(1)}, bf16[256,256]{1,0:T(8,128)(2,1)S(1)}, u32[]{:S(2)}, u32[]{:S(2)}) collective-permute-start(bf16[256,256]{1,0:T(8,128)(2,1)S(1)} %get-tuple-element.44), channel_id=1, source_target_pairs={{0,3},{1,2},{2,1},{3,0},{4,7},{5,6},{6,5},{7,4},{8,11},{9,10},{10,... | collective-permute-start | bytes 393224 | tf_op jit(solution)/shard_map/ppermute | solution.py:181
  95.3 3.2 %collective-permute-start.6 = (bf16[256,256]{1,0:T(8,128)(2,1)S(1)}, bf16[256,256]{1,0:T(8,128)(2,1)S(1)}, u32[]{:S(2)}, u32[]{:S(2)}) collective-permute-start(bf16[256,256]{1,0:T(8,128)(2,1)S(1)} %get-tuple-element.42), channel_id=1, source_target_pairs={{0,1},{1,0},{2,3},{3,2},{4,5},{5,4},{6,7},{7,6},{8,9},{9,8},{10,11... | collective-permute-start | bytes 393224 | tf_op jit(solution)/shard_map/ppermute | solution.py:181
